TPU v7x, 32 devices: a whole 2x2x4 slice. The times are simulated.
32 devices in a mesh: ens: 2 (over x), mode: 16 (over z, y, core).
Axes of the slice: x: 2, y: 2, z: 4, core: 2. Of those that a mesh axis runs over, the one named last changes fastest.
Arguments:
- velocity: float32 [6, 512, 2048], P('ens', 'mode'), parts along dimension 0, may hold values from -4 to 4
- log_conf: float32 [12, 512, 2048], P('ens', 'mode'), parts along dimension 0, may hold values from -3 to 3
- orientation: int32 [32], replicated, may hold values from 0 to 7
- wall_speed: float32 [2], P('ens'), parts along dimension 0, may hold values from 0.5 to 2
Outputs:
- vel_next: float32 [6, 512, 2048], P('ens', 'mode'), parts along dimension 0
- logc_next: float32 [12, 512, 2048], P('ens', 'mode'), parts along dimension 0
There are 2 independent parts, one for each index of `ens`. A program takes and returns all parts, laid end to end along the dimension named above; an argument that names none is the same for every part. Nothing has to cross between parts.
All inputs are finite; a program needn't handle non-finite values.
Results may differ from a plain program's by a relative error of at most 0.0003.
Values sent between devices are 32-bit elements; how exact they have to be, the bound alone decides.
A program may use at most 512 MiB of HBM per device.

v0:
```python
import functools

import jax
import jax.numpy as jnp
import ml_dtypes
import numpy as np
from jax import lax
from jax.experimental import pallas as pl
from jax.experimental.pallas import tpu as pltpu
from jax.sharding import PartitionSpec as P

NODE_1D = 8
CYCLES = 2
PLANES = 512
LANES = CYCLES * NODE_1D * NODE_1D
STEP_DT = 0.002
RELAX_TIME = 0.02
MOBILITY = 0.3
LAYER_HEIGHT = 0.25
R_INNER = 1.0
ROWS = 16
BF = jnp.bfloat16
F32 = jnp.float32
MESH = pl.DeviceIdType.MESH


def cheb_table(points):
    nodes_xi = -np.cos(np.pi * np.arange(points) / (points - 1))
    weights = np.ones(points)
    weights[0] = 2.0
    weights[-1] = 2.0
    weights = weights * (-1.0) ** np.arange(points)
    identity = np.eye(points)
    spacing = nodes_xi[:, None] - nodes_xi[None, :] + identity
    matrix = weights[:, None] / weights[None, :] / spacing
    matrix = matrix * (1.0 - identity)
    matrix = matrix - identity * matrix.sum(axis=1)[:, None]
    return (nodes_xi, matrix)


def halves(table):
    high = np.asarray(table, np.float32).astype(ml_dtypes.bfloat16)
    low = (np.asarray(table, np.float64) - high.astype(np.float64)).astype(ml_dtypes.bfloat16)
    return high, low


def tables():
    n = np.arange(PLANES)
    k = np.arange(PLANES // 2)
    angle = (n[:, None] * k[None, :] % PLANES) * (2.0 * np.pi / PLANES)
    cosine = np.cos(angle) * np.sqrt(2.0 / PLANES)
    sine = np.sin(angle) * np.sqrt(2.0 / PLANES)
    cosine[:, 0] = PLANES**-0.5
    sine[:, 0] = (-1.0) ** n * PLANES**-0.5
    basis = np.stack([cosine, sine], axis=2).reshape(PLANES, PLANES)
    dbasis = np.stack([-k * sine, k * cosine], axis=2).reshape(PLANES, PLANES)
    forward = np.concatenate([basis, dbasis], axis=0)
    backward = np.concatenate([basis.T, -dbasis.T], axis=1)

    xi, matrix = cheb_table(NODE_1D)
    eye, eyes = np.eye(NODE_1D), np.eye(CYCLES)
    d_r = np.kron(eye, np.kron(eyes, matrix.T * (2.0 * CYCLES)))
    d_z = np.kron(matrix.T * (2.0 / LAYER_HEIGHT), np.eye(CYCLES * NODE_1D))
    mean = np.eye(CYCLES * NODE_1D)
    for c in range(1, CYCLES):
        i = c * NODE_1D
        mean[i - 1 : i + 1, i - 1 : i + 1] = 0.5
    mean = np.kron(eye, mean)
    weight = np.ones(NODE_1D)
    weight[0] = weight[-1] = 0.5
    weight = np.repeat(weight, CYCLES * NODE_1D)
    mean_w = mean * weight[None, :]
    both = np.concatenate([d_r, d_z], axis=1)
    grad = np.concatenate([d_r @ mean_w, d_z @ mean_w], axis=1)
    div = np.concatenate([d_r, d_z], axis=0)
    return (
        *halves(forward),
        *halves(backward),
        np.concatenate(
            [
                *halves(both),
                *halves(grad),
                *halves(div.reshape(2, LANES, LANES).transpose(1, 0, 2).reshape(LANES, -1)),
                mean_w.astype(ml_dtypes.bfloat16),
            ],
            axis=1,
        ),
    )


def inverse_radius(lane):
    xi, _ = cheb_table(NODE_1D)
    radius = R_INNER + (np.arange(CYCLES)[:, None] + (xi[None, :] + 1.0) / 2.0) / CYCLES
    total = jnp.zeros(lane.shape, F32)
    for i, r in enumerate(radius.reshape(-1)):
        total = jnp.where(lane % (CYCLES * NODE_1D) == i, float(1.0 / r), total)
    return total


def split(x):
    high = x.astype(BF)
    return high, (x - high.astype(F32)).astype(BF)


def dot(a, b):
    return jnp.dot(a, b, preferred_element_type=F32)


def dot3(ah, al, bh, bl):
    return dot(ah, bh) + (dot(ah, bl) + dot(al, bh))


def stored_of_grid(o, e, grid):
    side = NODE_1D
    y = grid // (CYCLES * side)
    x = grid % side
    swapped = o // 4 % 2 == 1
    a = jnp.where(swapped, x, y)
    b = jnp.where(swapped, y, x)
    a = jnp.where(o % 2 == 1, side - 1 - a, a)
    b = jnp.where(o // 2 % 2 == 1, side - 1 - b, b)
    return e * side * side + a * side + b


def stored_index(orient_ref, layer, grid):
    cycle = grid // NODE_1D % CYCLES
    place = jnp.zeros_like(grid)
    for c in range(CYCLES):
        o = orient_ref[layer * CYCLES + c]
        place = jnp.where(cycle == c, stored_of_grid(o, c, grid), place)
    return place


def square(m):
    a, b, c, d, e, f = m
    bb, cc, ee = b * b, c * c, e * e
    return (
        a * a + bb + cc,
        b * (a + d) + c * e,
        c * (a + f) + b * e,
        bb + d * d + ee,
        e * (d + f) + b * c,
        cc + ee + f * f,
    )


def product(m, n):
    a, b, c, d, e, f = m
    p, q, r, s, t, u = n
    return (
        a * p + b * q + c * r,
        a * q + b * s + c * t,
        a * r + b * t + c * u,
        b * q + d * s + e * t,
        b * r + d * t + e * u,
        c * r + e * t + f * u,
    )


def exponentials(psi):
    x = tuple(v * 0.125 for v in psi)
    x2 = square(x)
    x3 = product(x, x2)
    x4 = square(x2)
    even = [x2[i] * 0.5 + x4[i] * (1.0 / 24.0) for i in range(6)]
    for i in (0, 3, 5):
        even[i] = even[i] + 1.0
    odd = [x[i] + x3[i] * (1.0 / 6.0) for i in range(6)]
    plus = tuple(even[i] + odd[i] for i in range(6))
    minus = tuple(even[i] - odd[i] for i in range(6))
    for _ in range(3):
        plus, minus = square(plus), square(minus)
    return plus, minus


def field(ref, f, rows=slice(None)):
    return ref[rows, f * LANES : (f + 1) * LANES]


def main_kernel(
    n_dev, modes,
    vel_ref, logc_ref, orient_ref, fh_in, fl_in, bh_in, bl_in, node_in,
    out_ref,
    fh_ref, fl_ref, bh_ref, bl_ref, node_ref,
    xv, xp, xh, xl, vv, vp, dp, proj, face_out, face_in, part, sth, stl, div, rh, rl, back,
    local_sem, const_sem, vs_sem, vr_sem, ps_sem, pr_sem, fs_sem, fr_sem, bs_sem, br_sem,
):
    me = lax.axis_index("mode")
    up = lax.rem(me + 1, n_dev)
    down = lax.rem(me + n_dev - 1, n_dev)

    barrier = pltpu.get_barrier_semaphore()

    def greet(k, carry):
        pl.semaphore_signal(
            barrier, inc=1, device_id={"mode": lax.rem(me + k, n_dev)}, device_id_type=MESH
        )
        return carry

    lax.fori_loop(1, n_dev, greet, 0)
    pl.semaphore_wait(barrier, n_dev - 1)

    side = n_dev // 2
    half_of = me // side

    def target(k):
        j = k // 2
        return lax.rem(half_of + lax.rem(k, 2), 2) * side + lax.rem(me + j, side)

    def columns(d):
        return pl.ds(pl.multiple_of(d * LANES, LANES), LANES)

    def scatter(src_ref, dst, send, recv, k, to, slot):
        return pltpu.make_async_remote_copy(
            src_ref=src_ref.at[:, :, columns(to)],
            dst_ref=dst.at[slot],
            send_sem=send.at[k],
            recv_sem=recv.at[slot],
            device_id={"mode": to},
            device_id_type=MESH,
        )

    def send_all(src_ref, dst, send, recv):
        def step(k, carry):
            scatter(src_ref, dst, send, recv, k, target(k), me).start()
            return carry

        lax.fori_loop(1, n_dev, step, 0)

    def recv_all(src_ref, dst, send, recv):
        def step(k, carry):
            frm = target(k)
            scatter(src_ref, dst, send, recv, k, frm, frm).wait_recv()
            return carry

        lax.fori_loop(1, n_dev, step, 0)

    def sent_all(src_ref, dst, send, recv):
        def step(k, carry):
            scatter(src_ref, dst, send, recv, k, target(k), me).wait_send()
            return carry

        lax.fori_loop(1, n_dev, step, 0)

    send_all(vel_ref, xv, vs_sem, vr_sem)
    send_all(logc_ref, xp, ps_sem, pr_sem)
    own_v = pltpu.make_async_copy(vel_ref.at[:, :, columns(me)], xv.at[me], local_sem.at[0])
    own_p = pltpu.make_async_copy(logc_ref.at[:, :, columns(me)], xp.at[me], local_sem.at[1])
    own_v.start()
    own_p.start()
    loads = [
        pltpu.make_async_copy(a, b, const_sem.at[i])
        for i, (a, b) in enumerate(
            (
                (node_in, node_ref), (fh_in, fh_ref), (fl_in, fl_ref),
                (bh_in, bh_ref), (bl_in, bl_ref),
            )
        )
    ]
    for load in loads:
        load.start()

    stored = lax.broadcasted_iota(jnp.int32, (LANES, LANES), 0)
    grid = lax.broadcasted_iota(jnp.int32, (LANES, LANES), 1)
    to_grid = jnp.where(stored_index(orient_ref, me, grid) == stored, 1.0, 0.0).astype(BF)

    def permuted(src, count, base):
        for f in range(count):
            coeffs = src[:, f].reshape(PLANES, LANES)
            high, low = split(coeffs)
            at = slice((base + f) * LANES, (base + f + 1) * LANES)
            xh[:, at] = dot(high, to_grid).astype(BF)
            xl[:, at] = dot(low, to_grid).astype(BF)

    half = PLANES // 2
    lane = lax.broadcasted_iota(jnp.int32, (1, LANES), 1)
    inv_r = inverse_radius(lane)
    for load in loads[:3]:
        load.wait()
    wide = 2 * LANES
    both_h, both_l, grad_h, grad_l = [node_ref.at[:, i * wide : (i + 1) * wide] for i in range(4)]
    mean_ref = node_ref.at[:, 6 * wide : 6 * wide + LANES]

    own_v.wait()
    recv_all(vel_ref, xv, vs_sem, vr_sem)
    permuted(xv, 3, 0)

    def velocity_block(i, carry):
        at = pl.ds(pl.multiple_of(i * half, half), half)
        cols = slice(0, 3 * LANES)
        vv[at, :] = dot3(fh_ref[at, :], fl_ref[at, :], xh[:, cols], xl[:, cols])
        return carry

    lax.fori_loop(0, 4, velocity_block, 0)

    width = CYCLES * NODE_1D

    def grad_block(i, carry):
        block = half // 2
        at = pl.ds(pl.multiple_of(i * block, block), block)
        dth_at = pl.ds(pl.multiple_of(PLANES + i * block, block), block)
        u = [field(vv, f, at) for f in range(3)]
        dth = [field(vv, f, dth_at) for f in range(3)]
        hoop = [(dth[0] - u[1]) * inv_r, (dth[1] + u[0]) * inv_r, dth[2] * inv_r]
        for f in range(3):
            uh, ul = split(u[f])
            both = dot3(uh, ul, grad_h[...], grad_l[...])
            hh, hl = split(hoop[f])
            g = (both[:, :LANES], dot(hh, mean_ref[...]) + dot(hl, mean_ref[...]), both[:, LANES:])
            for j in range(3):
                c = 3 * f + j
                proj[at, c * LANES : (c + 1) * LANES] = g[j]
        return carry

    lax.fori_loop(0, 4, grad_block, 0)

    groups = LANES // width
    short = PLANES // groups
    for slot, start in ((0, LANES - width), (1, 0)):

        def pack(i, carry, slot=slot, start=start):
            at = pl.ds(pl.multiple_of(i * 64, 64), 64)
            total = jnp.zeros((64, LANES), F32)
            for c in range(groups):
                moved = field(proj, c, at)
                shift = (c * width - start) % LANES
                moved = pltpu.roll(moved, shift, 1) if shift else moved
                total = jnp.where(lane // width == c, moved, total)
            face_out[slot, at, :] = total
            return carry

        lax.fori_loop(0, PLANES // 64, pack, 0)
        total = jnp.zeros((short, LANES), F32)
        for b in range(groups):
            moved = field(proj, 8, slice(b * short, (b + 1) * short))
            shift = (b * width - start) % LANES
            moved = pltpu.roll(moved, shift, 1) if shift else moved
            total = jnp.where(lane // width == b, moved, total)
        face_out[slot, PLANES:, :] = total

    def face_copy(slot, to):
        return pltpu.make_async_remote_copy(
            src_ref=face_out.at[slot],
            dst_ref=face_in.at[slot],
            send_sem=fs_sem.at[slot],
            recv_sem=fr_sem.at[slot],
            device_id={"mode": to},
            device_id_type=MESH,
        )

    face_up, face_down = face_copy(0, up), face_copy(1, down)
    face_up.start()
    face_down.start()

    face_up.wait()
    face_down.wait()

    top = lane >= LANES - width
    low_rows = lane < width

    def unpacked(from_down, from_up, c):
        shift = (-c * width) % LANES
        below = pltpu.roll(from_down, shift, 1) if shift else from_down
        shift = (LANES - width - c * width) % LANES
        above = pltpu.roll(from_up, shift, 1) if shift else from_up
        return jnp.where(top, above, jnp.where(low_rows, below, 0.0))

    for b in range(groups):

        def face_block(i, carry, b=b):
            start = pl.multiple_of(b * short + i * ROWS, ROWS)
            at = pl.ds(start, ROWS)
            nine = pl.ds(pl.multiple_of(PLANES + i * ROWS, ROWS), ROWS)
            down_face, up_face = face_in[0, at, :], face_in[1, at, :]
            g = [field(proj, c, at) + unpacked(down_face, up_face, c) for c in range(8)]
            g.append(field(proj, 8, at) + unpacked(face_in[0, nine, :], face_in[1, nine, :], b))
            for c in range(9):
                proj[at, c * LANES : (c + 1) * LANES] = g[c]
            u = [field(vv, f, at) for f in range(3)]
            for f in range(3):
                conv = g[3 * f] * u[0] + g[3 * f + 1] * u[1] + g[3 * f + 2] * u[2]
                div[at, f * LANES : (f + 1) * LANES] = -conv
            return carry

        lax.fori_loop(0, short // ROWS, face_block, 0)

    def recv_half(far):
        def step(k, carry):
            frm = target(2 * k + far)
            scatter(logc_ref, xp, ps_sem, pr_sem, 2 * k + far, frm, frm).wait_recv()
            return carry

        lax.fori_loop(1 - far, side, step, 0)

    def conf_half(far):
        which = lax.rem(half_of + far, 2)
        rows = pl.ds(pl.multiple_of(which * half, half), half)
        for f in range(6):
            high, low = split(xp[pl.ds(which * side, side), f].reshape(half, LANES))
            at = slice((3 + f) * LANES, (4 + f) * LANES)
            xh[rows, at] = dot(high, to_grid).astype(BF)
            xl[rows, at] = dot(low, to_grid).astype(BF)
        for part_of in range(3):
            cols = slice((3 + 2 * part_of) * LANES, (5 + 2 * part_of) * LANES)
            dst = slice(2 * part_of * LANES, (2 * part_of + 2) * LANES)

            def conf_block(i, carry, cols=cols, dst=dst):
                at = pl.ds(pl.multiple_of(i * PLANES, PLANES), PLANES)
                total = dot3(fh_ref[at, rows], fl_ref[at, rows], xh[rows, cols], xl[rows, cols])
                vp[at, dst] = vp[at, dst] + total if far else total
                return carry

            lax.fori_loop(0, 2, conf_block, 0)

    own_p.wait()
    recv_half(0)
    conf_half(0)
    recv_half(1)
    conf_half(1)

    def deriv_block(i, carry):
        at = pl.ds(pl.multiple_of(i * half, half), half)
        for m in range(6):
            ph, pw = split(field(vp, m, at))
            dp[at, 2 * m * LANES : (2 * m + 2) * LANES] = dot3(ph, pw, both_h[...], both_l[...])
        return carry

    lax.fori_loop(0, 2, deriv_block, 0)

    def put_rate(at, f, value):
        high, low = split(value)
        rh[at, f * LANES : (f + 1) * LANES] = high
        rl[at, f * LANES : (f + 1) * LANES] = low

    diag = (0, 3, 5)

    def local_block(i, carry):
        at = pl.ds(pl.multiple_of(i * ROWS, ROWS), ROWS)
        dth_at = pl.ds(pl.multiple_of(PLANES + i * ROWS, ROWS), ROWS)
        u_r, u_t, u_z = [field(vv, f, at) for f in range(3)]
        psi = [field(vp, m, at) for m in range(6)]
        conform, inverse = exponentials(psi)
        spin = u_t * inv_r
        curve = [-2.0 * psi[1], psi[0] - psi[3], -psi[4], 2.0 * psi[1], psi[2], None]
        for m in range(6):
            dth = field(vp, m, dth_at)
            if curve[m] is not None:
                dth = dth + curve[m]
            total = u_r * field(dp, 2 * m, at) + spin * dth + u_z * field(dp, 2 * m + 1, at)
            unit = 1.0 if m in diag else 0.0
            relax = (1.0 / RELAX_TIME) * (
                unit
                - inverse[m]
                + MOBILITY * (conform[m] - 2.0 * unit + inverse[m])
            )
            part[at, m * LANES : (m + 1) * LANES] = -(total + relax)
        stress = [conform[m] - 1.0 if m in diag else conform[m] for m in range(6)]
        for f, m in enumerate((0, 2, 1, 4, 2, 5)):
            high, low = split(stress[m])
            sth[at, f * LANES : (f + 1) * LANES] = high
            stl[at, f * LANES : (f + 1) * LANES] = low
        hoop_rt = stress[1] * inv_r
        put_rate(at, 9, hoop_rt)
        put_rate(at, 10, stress[3] * inv_r)
        put_rate(at, 11, stress[4] * inv_r)
        div[at, 0:LANES] += (stress[0] - stress[3]) * inv_r
        div[at, LANES : 2 * LANES] += 2.0 * hoop_rt
        div[at, 2 * LANES : 3 * LANES] += stress[2] * inv_r
        return carry

    lax.fori_loop(0, PLANES // ROWS, local_block, 0)

    def div_block(i, carry):
        at = pl.ds(pl.multiple_of(i * half, half), half)
        for f in range(3):
            dst = slice(f * LANES, (f + 1) * LANES)
            total = div[at, dst]
            for j in range(2):
                cols = slice((2 * f + j) * LANES, (2 * f + j + 1) * LANES)
                node = slice(4 * wide + j * LANES, 4 * wide + (j + 1) * LANES)
                node_low = slice(5 * wide + j * LANES, 5 * wide + (j + 1) * LANES)
                total = total + dot3(sth[at, cols], stl[at, cols], node_ref[:, node], node_ref[:, node_low])
            div[at, dst] = total
        return carry

    lax.fori_loop(0, 2, div_block, 0)

    def join_block(i, carry):
        at = pl.ds(pl.multiple_of(i * ROWS, ROWS), ROWS)
        g = [field(proj, c, at) for c in range(9)]
        psi = [field(vp, m, at) for m in range(6)]
        for f in range(3):
            put_rate(at, f, field(div, f, at))
        wa, wb, wc = 0.5 * (g[1] - g[3]), 0.5 * (g[2] - g[6]), 0.5 * (g[5] - g[7])
        p0 = (psi[0], psi[1], psi[2])
        p1 = (psi[1], psi[3], psi[4])
        p2 = (psi[2], psi[4], psi[5])
        r0 = [wa * p1[j] + wb * p2[j] for j in range(3)]
        r1 = [wc * p2[j] - wa * p0[j] for j in range(3)]
        r2 = [-(wb * p0[j] + wc * p1[j]) for j in range(3)]
        sums = (
            2.0 * (r0[0] + g[0]),
            r0[1] + r1[0] + (g[1] + g[3]),
            r0[2] + r2[0] + (g[2] + g[6]),
            2.0 * (r1[1] + g[4]),
            r1[2] + r2[1] + (g[5] + g[7]),
            2.0 * (r2[2] + g[8]),
        )
        for m in range(6):
            put_rate(at, 3 + m, field(part, m, at) + sums[m])
        return carry

    lax.fori_loop(0, PLANES // ROWS, join_block, 0)

    share = PLANES // 4
    per = share // modes

    def put_back(i, f, count, value):
        for j in range(count):
            back[pl.ds(i * per, per), f + j] = value[:, j * LANES : (j + 1) * LANES].reshape(
                per, modes, LANES
            )

    def give(to, slot):
        return pltpu.make_async_remote_copy(
            src_ref=back.at[to],
            dst_ref=out_ref.at[slot],
            send_sem=bs_sem.at[to],
            recv_sem=br_sem.at[slot],
            device_id={"mode": to},
            device_id_type=MESH,
        )

    for load in loads[3:]:
        load.wait()

    quarter = me // per

    def back_block(step, carry):
        pair = lax.rem(quarter // 2 + 1 + step // 2, 2)
        i = pair * 2 + lax.rem(quarter + step + step // 2, 2)
        at = pl.ds(pl.multiple_of(i * share, share), share)
        cols, hoops = slice(0, 3 * LANES), slice(9 * LANES, 12 * LANES)
        total = dot3(bh_ref[at, :PLANES], bl_ref[at, :PLANES], rh[:, cols], rl[:, cols])
        total += dot3(bh_ref[at, PLANES:], bl_ref[at, PLANES:], rh[:, hoops], rl[:, hoops])
        put_back(i, 0, 3, total)
        for f in (3, 6):
            cols = slice(f * LANES, (f + 3) * LANES)
            total = dot3(bh_ref[at, :PLANES], bl_ref[at, :PLANES], rh[:, cols], rl[:, cols])
            put_back(i, f, 3, total)

        def give_start(j, inner):
            to = i * per + lax.rem(me + j, per)

            @pl.when(to != me)
            def _():
                give(to, me).start()

            return inner

        lax.fori_loop(0, per, give_start, 0)
        return carry

    lax.fori_loop(0, 4, back_block, 0)
    own = pltpu.make_async_copy(back.at[me], out_ref.at[me], local_sem.at[0])
    own.start()
    sent_all(vel_ref, xv, vs_sem, vr_sem)
    sent_all(logc_ref, xp, ps_sem, pr_sem)
    own.wait()

    def give_wait(k, carry):
        to = target(k)
        give(to, to).wait_recv()
        give(to, me).wait_send()
        return carry

    lax.fori_loop(1, n_dev, give_wait, 0)


def final_kernel(
    n_dev, modes, group, orient_ref, wall_ref, below_ref, rates_ref, above_ref, mean_ref, vel_ref, logc_ref,
    vel_out, logc_out,
):
    step = pl.program_id(0)
    me = lax.axis_index("mode")
    width = CYCLES * NODE_1D
    lane = lax.broadcasted_iota(jnp.int32, (1, LANES), 1)
    top = lane >= LANES - width
    low_rows = lane < width
    grid = lax.broadcasted_iota(jnp.int32, (LANES, LANES), 0)
    stored = lax.broadcasted_iota(jnp.int32, (LANES, LANES), 1)
    mode_ids = me * modes + lax.broadcasted_iota(jnp.int32, (modes, 1), 0)
    speed = jnp.where(mode_ids == 0, wall_ref[0], 0.0)
    cycle = lane // (NODE_1D * NODE_1D)
    lead = lane // NODE_1D % NODE_1D
    trail = lane % NODE_1D
    fields = 9 if modes % 8 == 0 else 1
    rows = fields * modes
    for g in range(group):
        layer = step * group + g
        hot = jnp.where(stored_index(orient_ref, layer, grid) == stored, 1.0, 0.0).astype(BF)
        hot = dot(mean_ref[...], hot).astype(BF)
        hot = jnp.concatenate([hot, hot], axis=0)
        code = jnp.zeros_like(lane)
        for c in range(CYCLES):
            code = jnp.where(cycle == c, orient_ref[layer * CYCLES + c], code)
        flipped_a = jnp.where(code % 2 == 1, NODE_1D - 1 - lead, lead)
        flipped_b = jnp.where(code // 2 % 2 == 1, NODE_1D - 1 - trail, trail)
        x = jnp.where(code // 4 % 2 == 1, flipped_a, flipped_b)
        inner = jnp.logical_and(cycle == 0, x == 0)
        outer = jnp.logical_and(cycle == CYCLES - 1, x == NODE_1D - 1)
        on_wall = jnp.logical_or(inner, outer)
        cols = slice(g * LANES, (g + 1) * LANES)

        def part_of(ref, at, f):
            return ref[at, f : f + fields].reshape(rows, LANES)

        for f in range(0, 9, fields):
            rate = part_of(rates_ref, g, f)
            below = part_of(rates_ref, g - 1, f) if g else part_of(below_ref, 0, f)
            above = part_of(rates_ref, g + 1, f) if g < group - 1 else part_of(above_ref, 0, f)
            other = pltpu.roll(below, width, 1)
            other = jnp.where(low_rows, other, pltpu.roll(above, LANES - width, 1))
            rate = jnp.where(jnp.logical_or(top, low_rows), 0.5 * (rate + other), rate)
            high, low = split(rate)
            rate = STEP_DT * dot(jnp.concatenate([high, low], axis=1), hot)
            for j in range(fields):
                c = f + j
                own = rate[j * modes : (j + 1) * modes]
                if c < 3:
                    wall = jnp.where(inner, speed, 0.0) if c == 1 else 0.0
                    vel_out[c, :, cols] = jnp.where(on_wall, wall, vel_ref[c, :, cols] + own)
                else:
                    logc_out[c - 3, :, cols] = logc_ref[c - 3, :, cols] + own


def body(velocity, log_conf, orientation, wall_speed):
    n_dev = lax.axis_size("mode")
    modes = velocity.shape[1]
    consts = [jnp.asarray(t) for t in tables()]
    hbm = pl.BlockSpec(memory_space=pl.ANY)
    smem = pl.BlockSpec(memory_space=pltpu.SMEM)
    dma = pltpu.SemaphoreType.DMA
    face_rows = PLANES + PLANES * CYCLES * NODE_1D // LANES
    rates = pl.pallas_call(
        functools.partial(main_kernel, n_dev, modes),
        out_shape=jax.ShapeDtypeStruct((n_dev, 9, modes, LANES), F32),
        in_specs=[hbm, hbm, smem] + [hbm] * len(consts),
        out_specs=hbm,
        scratch_shapes=[pltpu.VMEM(t.shape, t.dtype) for t in consts]
        + [
            pltpu.VMEM((n_dev, 3, modes, LANES), F32),
            pltpu.VMEM((n_dev, 6, modes, LANES), F32),
            pltpu.VMEM((PLANES, 9 * LANES), BF),
            pltpu.VMEM((PLANES, 9 * LANES), BF),
            pltpu.VMEM((2 * PLANES, 3 * LANES), F32),
            pltpu.VMEM((2 * PLANES, 6 * LANES), F32),
            pltpu.VMEM((PLANES, 12 * LANES), F32),
            pltpu.VMEM((PLANES, 9 * LANES), F32),
            pltpu.VMEM((2, face_rows, LANES), F32),
            pltpu.VMEM((2, face_rows, LANES), F32),
            pltpu.VMEM((PLANES, 6 * LANES), F32),
            pltpu.VMEM((PLANES, 6 * LANES), BF),
            pltpu.VMEM((PLANES, 6 * LANES), BF),
            pltpu.VMEM((PLANES, 3 * LANES), F32),
            pltpu.VMEM((PLANES, 12 * LANES), BF),
            pltpu.VMEM((PLANES, 12 * LANES), BF),
            pltpu.VMEM((n_dev, 9, modes, LANES), F32),
            dma((2,)),
            dma((len(consts),)),
            dma((n_dev,)),
            dma((n_dev,)),
            dma((n_dev,)),
            dma((n_dev,)),
            dma((2,)),
            dma((2,)),
            dma((n_dev,)),
            dma((n_dev,)),
        ],
        compiler_params=pltpu.CompilerParams(
            collective_id=0, has_side_effects=True, vmem_limit_bytes=60 * 2**20
        ),
        name="fields",
    )(velocity, log_conf, orientation, *consts)

    group = 8
    mean = jnp.asarray(mean_table().astype(ml_dtypes.bfloat16))
    tile = group * LANES
    return pl.pallas_call(
        functools.partial(final_kernel, n_dev, modes, group),
        grid=(n_dev // group,),
        out_shape=(
            jax.ShapeDtypeStruct(velocity.shape, F32),
            jax.ShapeDtypeStruct(log_conf.shape, F32),
        ),
        in_specs=[
            smem,
            smem,
            pl.BlockSpec((1, 9, modes, LANES), lambda i: (lax.rem(i * group + n_dev - 1, n_dev), 0, 0, 0)),
            pl.BlockSpec((group, 9, modes, LANES), lambda i: (i, 0, 0, 0)),
            pl.BlockSpec((1, 9, modes, LANES), lambda i: (lax.rem(i * group + group, n_dev), 0, 0, 0)),
            pl.BlockSpec((LANES, LANES), lambda i: (0, 0)),
            pl.BlockSpec((3, modes, tile), lambda i: (0, 0, i)),
            pl.BlockSpec((6, modes, tile), lambda i: (0, 0, i)),
        ],
        out_specs=(
            pl.BlockSpec((3, modes, tile), lambda i: (0, 0, i)),
            pl.BlockSpec((6, modes, tile), lambda i: (0, 0, i)),
        ),
        compiler_params=pltpu.CompilerParams(vmem_limit_bytes=60 * 2**20),
        name="finish",
    )(orientation, wall_speed, rates, rates, rates, mean, velocity, log_conf)


def mean_table():
    mean = np.eye(CYCLES * NODE_1D, dtype=np.float32)
    for c in range(1, CYCLES):
        i = c * NODE_1D
        mean[i - 1 : i + 1, i - 1 : i + 1] = 0.5
    return np.kron(np.eye(NODE_1D, dtype=np.float32), mean)


def solution(mesh):
    in_specs = (P("ens", "mode", None), P("ens", "mode", None), P(), P("ens"))
    out_specs = (P("ens", "mode", None), P("ens", "mode", None))
    return jax.shard_map(body, mesh=mesh, in_specs=in_specs, out_specs=out_specs, check_vma=False)
```

profile of v0, /device:TPU:15, one launch (start us, length us, event | category | flops | bytes accessed | tf_op | source)
XLA Modules:
  0.0 127.4 jit_solution(14849783494695670365)
XLA Ops:
  1.3 120.7 %fields.1.below_ref.rates_ref.above_ref = f32[16,9,32,128]{3,2,1,0:T(8,128)} custom-call(f32[3,32,2048]{2,1,0:T(8,128)} %vel_ref.3, f32[6,32,2048]{2,1,0:T(8,128)} %logc_ref.3, s32[32]{0:T(128)} %orient_ref.3, bf16[1024,512]{1,0:T(8,128)(2,1)} %constant.12.clone.fh_in, bf16[1024,512]{1,0:T(8,128)(2,1)} %constant.13.clone.fl_in, ...), custom_call_target="tpu_custom_call" | custom-call | tf_op jit(solution)/shard_map/fields/pallas_call | solution.py:645
  121.9 5.5 %finish.1 = (f32[3,32,2048]{2,1,0:T(8,128)}, f32[6,32,2048]{2,1,0:T(8,128)}) custom-call(s32[32]{0:T(128)} %orient_ref.3, f32[1]{0:T(128)S(6)} %copy.12.wall_ref, f32[16,9,32,128]{3,2,1,0:T(8,128)} %fields.1.below_ref.rates_ref.above_ref, f32[16,9,32,128]{3,2,1,0:T(8,128)} %fields.1.below_ref.rates_ref.above_ref, ...), custom_call_target="tpu_custom_call" | custom-call | tf_op jit(solution)/shard_map/finish/pallas_call | solution.py:689
where the time goes:
time: 128 us; the launch traced here: 127 us
  Pallas kernels  126 us (98%)
  between operations  1.28 us (1%)
    pallas_call x1, Pallas kernels, body(): pl.pallas_call(functools.partial(main_kernel, n_dev, modes), out_shape=ja...  121 us
    pallas_call x1, Pallas kernels, body(): pl.pallas_call(functools.partial(final_kernel, n_dev, modes, group), grid...  5.46 us

commit v1 on v0

v1 whole, which is shorter than its diff:
```python
import functools

import jax
import jax.numpy as jnp
import ml_dtypes
import numpy as np
from jax import lax
from jax.experimental import pallas as pl
from jax.experimental.pallas import tpu as pltpu
from jax.sharding import PartitionSpec as P

NODE_1D = 8
CYCLES = 2
PLANES = 512
CELL = NODE_1D * NODE_1D
LANES = CYCLES * CELL
KEPT = CELL - NODE_1D
SLOT_OF = (0, 1, 2, 4, 5, 6, 7, 8, 3)
STEP_DT = 0.002
RELAX_TIME = 0.02
MOBILITY = 0.3
LAYER_HEIGHT = 0.25
R_INNER = 1.0
ROWS = 16
BF = jnp.bfloat16
F32 = jnp.float32
MESH = pl.DeviceIdType.MESH


def cheb_table(points):
    nodes_xi = -np.cos(np.pi * np.arange(points) / (points - 1))
    weights = np.ones(points)
    weights[0] = 2.0
    weights[-1] = 2.0
    weights = weights * (-1.0) ** np.arange(points)
    identity = np.eye(points)
    spacing = nodes_xi[:, None] - nodes_xi[None, :] + identity
    matrix = weights[:, None] / weights[None, :] / spacing
    matrix = matrix * (1.0 - identity)
    matrix = matrix - identity * matrix.sum(axis=1)[:, None]
    return (nodes_xi, matrix)


def halves(table):
    high = np.asarray(table, np.float32).astype(ml_dtypes.bfloat16)
    low = (np.asarray(table, np.float64) - high.astype(np.float64)).astype(ml_dtypes.bfloat16)
    return high, low


def tables():
    n = np.arange(PLANES)
    k = np.arange(PLANES // 2)
    angle = (n[:, None] * k[None, :] % PLANES) * (2.0 * np.pi / PLANES)
    cosine = np.cos(angle) * np.sqrt(2.0 / PLANES)
    sine = np.sin(angle) * np.sqrt(2.0 / PLANES)
    cosine[:, 0] = PLANES**-0.5
    sine[:, 0] = (-1.0) ** n * PLANES**-0.5
    basis = np.stack([cosine, sine], axis=2).reshape(PLANES, PLANES)
    dbasis = np.stack([-k * sine, k * cosine], axis=2).reshape(PLANES, PLANES)
    forward = np.concatenate([basis, dbasis], axis=0)
    backward = np.concatenate([basis.T, -dbasis.T], axis=1)

    xi, matrix = cheb_table(NODE_1D)
    eye, eyes = np.eye(NODE_1D), np.eye(CYCLES)
    cell_r = np.kron(matrix.T * (2.0 * CYCLES), eye)
    cell_z = np.kron(eye, matrix.T * (2.0 / LAYER_HEIGHT))
    d_r, d_z = np.kron(eyes, cell_r), np.kron(eyes, cell_z)
    mean = np.eye(CYCLES * NODE_1D)
    for c in range(1, CYCLES):
        i = c * NODE_1D
        mean[i - 1 : i + 1, i - 1 : i + 1] = 0.5
    mean = np.kron(mean, eye)
    weight = np.ones(NODE_1D)
    weight[0] = weight[-1] = 0.5
    weight = np.tile(weight, CYCLES * NODE_1D)
    mean_w = mean * weight[None, :]
    both = np.concatenate([d_r, d_z], axis=1)
    grad = np.concatenate([d_r @ mean_w, d_z @ mean_w], axis=1)
    div = np.kron(np.eye(2), np.concatenate([cell_r, cell_z], axis=0))
    return (
        *halves(forward),
        *halves(backward),
        np.concatenate([*halves(both), *halves(grad), mean_w.astype(ml_dtypes.bfloat16)], axis=1),
        np.concatenate(halves(div), axis=1),
    )


def inverse_radius(lane):
    xi, _ = cheb_table(NODE_1D)
    radius = R_INNER + (np.arange(CYCLES)[:, None] + (xi[None, :] + 1.0) / 2.0) / CYCLES
    total = jnp.zeros(lane.shape, F32)
    for i, r in enumerate(radius.reshape(-1)):
        total = jnp.where(lane // NODE_1D == i, float(1.0 / r), total)
    return total


def split(x):
    high = x.astype(BF)
    return high, (x - high.astype(F32)).astype(BF)


def dot(a, b):
    return jnp.dot(a, b, preferred_element_type=F32)


def dot3(ah, al, bh, bl):
    return dot(ah, bh) + (dot(ah, bl) + dot(al, bh))


def stored_of_grid(o, grid):
    side = NODE_1D
    y = grid % side
    x = grid // side % side
    swapped = o // 4 % 2 == 1
    a = jnp.where(swapped, x, y)
    b = jnp.where(swapped, y, x)
    a = jnp.where(o % 2 == 1, side - 1 - a, a)
    b = jnp.where(o // 2 % 2 == 1, side - 1 - b, b)
    return a * side + b


def stored_index(orient_ref, layer, grid):
    cycle = grid // CELL
    place = jnp.zeros_like(grid)
    for c in range(CYCLES):
        o = orient_ref[layer * CYCLES + c]
        place = jnp.where(cycle == c, c * CELL + stored_of_grid(o, grid), place)
    return place


def square(m):
    a, b, c, d, e, f = m
    bb, cc, ee = b * b, c * c, e * e
    return (
        a * a + bb + cc,
        b * (a + d) + c * e,
        c * (a + f) + b * e,
        bb + d * d + ee,
        e * (d + f) + b * c,
        cc + ee + f * f,
    )


def product(m, n):
    a, b, c, d, e, f = m
    p, q, r, s, t, u = n
    return (
        a * p + b * q + c * r,
        a * q + b * s + c * t,
        a * r + b * t + c * u,
        b * q + d * s + e * t,
        b * r + d * t + e * u,
        c * r + e * t + f * u,
    )


def exponentials(psi):
    x = tuple(v * 0.125 for v in psi)
    x2 = square(x)
    x3 = product(x, x2)
    x4 = square(x2)
    even = [x2[i] * 0.5 + x4[i] * (1.0 / 24.0) for i in range(6)]
    for i in (0, 3, 5):
        even[i] = even[i] + 1.0
    odd = [x[i] + x3[i] * (1.0 / 6.0) for i in range(6)]
    plus = tuple(even[i] + odd[i] for i in range(6))
    minus = tuple(even[i] - odd[i] for i in range(6))
    for _ in range(3):
        plus, minus = square(plus), square(minus)
    return plus, minus


def field(ref, f, rows=slice(None)):
    return ref[rows, f * LANES : (f + 1) * LANES]


def main_kernel(
    n_dev, modes, fold,
    vel_ref, logc_ref, orient_ref, fh_in, fl_in, bh_in, bl_in, node_in, div_in,
    out0_ref, out1_ref,
    fh_ref, fl_ref, bh_ref, bl_ref, node_ref, div_ref,
    raw, packed, xv, xp, xh, xl, ph, pw, vv, vp, dp, proj, face_out, face_in, conv, mom, sth, stl, rh, rl,
    kept, back0, back1,
    local_sem, const_sem, vs_sem, vr_sem, ps_sem, pr_sem, fs_sem, fr_sem, bs_sem, br_sem,
):
    me = lax.axis_index("mode")
    up = lax.rem(me + 1, n_dev)
    down = lax.rem(me + n_dev - 1, n_dev)

    barrier = pltpu.get_barrier_semaphore()

    def greet(k, carry):
        pl.semaphore_signal(
            barrier, inc=1, device_id={"mode": lax.rem(me + k, n_dev)}, device_id_type=MESH
        )
        return carry

    lax.fori_loop(1, n_dev, greet, 0)
    load_logc = pltpu.make_async_copy(logc_ref, raw, local_sem.at[0])
    load_logc.start()
    pl.semaphore_wait(barrier, n_dev - 1)

    side = n_dev // 2
    half_of = me // side

    def target(k):
        j = k // 2
        return lax.rem(half_of + lax.rem(k, 2), 2) * side + lax.rem(me + j, side)

    def columns(d):
        return pl.ds(pl.multiple_of(d * LANES, LANES), LANES)

    def every(do):
        def step(k, carry):
            do(k, target(k))
            return carry

        lax.fori_loop(1, n_dev, step, 0)

    def send_v(k, to, slot):
        return pltpu.make_async_remote_copy(
            src_ref=vel_ref.at[:, :, columns(to)],
            dst_ref=xv.at[slot],
            send_sem=vs_sem.at[k],
            recv_sem=vr_sem.at[slot],
            device_id={"mode": to},
            device_id_type=MESH,
        )

    def send_p(c, k, to, slot):
        return pltpu.make_async_remote_copy(
            src_ref=packed.at[c, to],
            dst_ref=xp.at[c, slot],
            send_sem=ps_sem.at[c, k],
            recv_sem=pr_sem.at[c, slot],
            device_id={"mode": to},
            device_id_type=MESH,
        )

    every(lambda k, to: send_v(k, to, me).start())
    own_v = pltpu.make_async_copy(vel_ref.at[:, :, columns(me)], xv.at[me], local_sem.at[1])
    own_v.start()
    loads = [
        pltpu.make_async_copy(a, b, const_sem.at[i])
        for i, (a, b) in enumerate(
            (
                (node_in, node_ref), (fh_in, fh_ref), (fl_in, fl_ref),
                (div_in, div_ref), (bh_in, bh_ref), (bl_in, bl_ref),
            )
        )
    ]
    for load in loads:
        load.start()

    lane = lax.broadcasted_iota(jnp.int32, (1, LANES), 1)
    lo = lane < CELL

    def swap(value):
        return pltpu.roll(value, CELL, 1)

    def pair_up(c, a, b):
        return jnp.where(lo, a, swap(b)) if c == 0 else jnp.where(lo, swap(a), b)

    load_logc.wait()
    own_p = [
        pltpu.make_async_copy(packed.at[c, me], xp.at[c, me], local_sem.at[2 + c]) for c in range(2)
    ]
    for c in range(2):

        def pack_psi(to, carry, c=c):
            at = columns(to)
            for p in range(3):
                packed[c, to, p] = pair_up(c, raw[2 * p, :, at], raw[2 * p + 1, :, at])
            return carry

        lax.fori_loop(0, n_dev, pack_psi, 0)
        every(lambda k, to, c=c: send_p(c, k, to, me).start())
        own_p[c].start()

    stored = lax.broadcasted_iota(jnp.int32, (LANES, LANES), 0)
    grid = lax.broadcasted_iota(jnp.int32, (LANES, LANES), 1)
    to_grid = jnp.where(stored_index(orient_ref, me, grid) == stored, 1.0, 0.0).astype(BF)

    half = PLANES // 2
    inv_r = inverse_radius(lane)
    for load in loads[:3]:
        load.wait()
    wide = 2 * LANES
    both_h, both_l, grad_h, grad_l = [node_ref.at[:, i * wide : (i + 1) * wide] for i in range(4)]
    mean_ref = node_ref.at[:, 4 * wide : 4 * wide + LANES]

    own_v.wait()
    every(lambda k, frm: send_v(k, frm, frm).wait_recv())
    for f in range(3):
        high, low = split(xv[:, f].reshape(PLANES, LANES))
        at = slice(f * LANES, (f + 1) * LANES)
        xh[:, at] = dot(high, to_grid).astype(BF)
        xl[:, at] = dot(low, to_grid).astype(BF)

    def velocity_block(i, carry):
        at = pl.ds(pl.multiple_of(i * half, half), half)
        vv[at, :] = dot3(fh_ref[at, :], fl_ref[at, :], xh[...], xl[...])
        return carry

    lax.fori_loop(0, 4, velocity_block, 0)

    def grad_block(i, carry):
        block = half // 2
        at = pl.ds(pl.multiple_of(i * block, block), block)
        dth_at = pl.ds(pl.multiple_of(PLANES + i * block, block), block)
        u = [field(vv, f, at) for f in range(3)]
        dth = [field(vv, f, dth_at) for f in range(3)]
        hoop = [(dth[0] - u[1]) * inv_r, (dth[1] + u[0]) * inv_r, dth[2] * inv_r]
        for f in range(3):
            uh, ul = split(u[f])
            both = dot3(uh, ul, grad_h[...], grad_l[...])
            hh, hl = split(hoop[f])
            g = (both[:, :LANES], dot(hh, mean_ref[...]) + dot(hl, mean_ref[...]), both[:, LANES:])
            for j in range(3):
                c = 3 * f + j
                proj[at, c * LANES : (c + 1) * LANES] = g[j]
        return carry

    lax.fori_loop(0, 4, grad_block, 0)

    groups = NODE_1D
    short = PLANES // groups

    def rolled(value, shift):
        return pltpu.roll(value, shift % LANES, 1) if shift % LANES else value

    def face_copy(slot, to):
        return pltpu.make_async_remote_copy(
            src_ref=face_out.at[slot],
            dst_ref=face_in.at[slot],
            send_sem=fs_sem.at[slot],
            recv_sem=fr_sem.at[slot],
            device_id={"mode": to},
            device_id_type=MESH,
        )

    faces = (face_copy(0, up), face_copy(1, down))
    for slot, start in ((0, NODE_1D - 1), (1, 0)):

        def pack(i, carry, slot=slot, start=start):
            at = pl.ds(pl.multiple_of(i * 64, 64), 64)
            total = jnp.zeros((64, LANES), F32)
            for c in range(groups):
                total = jnp.where(lane % groups == c, rolled(field(proj, c, at), c - start), total)
            face_out[slot, at, :] = total
            return carry

        lax.fori_loop(0, PLANES // 64, pack, 0)
        total = jnp.zeros((short, LANES), F32)
        for b in range(groups):
            moved = field(proj, 8, slice(b * short, (b + 1) * short))
            total = jnp.where(lane % groups == b, rolled(moved, b - start), total)
        face_out[slot, PLANES:, :] = total
        faces[slot].start()

    for face in faces:
        face.wait()

    top = lane % NODE_1D == NODE_1D - 1
    low_rows = lane % NODE_1D == 0

    def unpacked(from_down, from_up, c):
        below = rolled(from_down, -c)
        above = rolled(from_up, NODE_1D - 1 - c)
        return jnp.where(top, above, jnp.where(low_rows, below, 0.0))

    for b in range(groups):

        def face_block(i, carry, b=b):
            start = pl.multiple_of(b * short + i * ROWS, ROWS)
            at = pl.ds(start, ROWS)
            nine = pl.ds(pl.multiple_of(PLANES + i * ROWS, ROWS), ROWS)
            down_face, up_face = face_in[0, at, :], face_in[1, at, :]
            g = [field(proj, c, at) + unpacked(down_face, up_face, c) for c in range(8)]
            g.append(field(proj, 8, at) + unpacked(face_in[0, nine, :], face_in[1, nine, :], b))
            for c in range(9):
                proj[at, c * LANES : (c + 1) * LANES] = g[c]
            u = [field(vv, f, at) for f in range(3)]
            for f in range(3):
                total = g[3 * f] * u[0] + g[3 * f + 1] * u[1] + g[3 * f + 2] * u[2]
                conv[at, f * LANES : (f + 1) * LANES] = -total
            return carry

        lax.fori_loop(0, short // ROWS, face_block, 0)

    def put_rate(at, f, value):
        high, low = split(value)
        rh[at, f * LANES : (f + 1) * LANES] = high
        rl[at, f * LANES : (f + 1) * LANES] = low

    share = PLANES // 4
    per = share // modes
    quarter = me // per
    backs, outs = (back0, back1), (out0_ref, out1_ref)
    diag = (0, 3, 5)

    def give(c, to, slot):
        return pltpu.make_async_remote_copy(
            src_ref=backs[c].at[to],
            dst_ref=outs[c].at[slot],
            send_sem=bs_sem.at[c, to],
            recv_sem=br_sem.at[c, slot],
            device_id={"mode": to},
            device_id_type=MESH,
        )

    def cycle_part(c):
        in_c = lo if c == 0 else jnp.logical_not(lo)
        o = orient_ref[me * CYCLES + c]
        same = stored // CELL == grid // CELL
        hit = jnp.logical_and(stored_of_grid(o, grid) == stored % CELL, same)
        cell_grid = jnp.where(hit, 1.0, 0.0).astype(BF)

        def conf_half(far):
            which = lax.rem(half_of + far, 2)
            rows = pl.ds(pl.multiple_of(which * half, half), half)
            for p in range(3):
                high, low = split(xp[c, pl.ds(which * side, side), p].reshape(half, LANES))
                at = slice(p * LANES, (p + 1) * LANES)
                ph[rows, at] = dot(high, cell_grid).astype(BF)
                pw[rows, at] = dot(low, cell_grid).astype(BF)

            def conf_block(i, carry):
                at = pl.ds(pl.multiple_of(i * half, half), half)
                total = dot3(fh_ref[at, rows], fl_ref[at, rows], ph[rows, :], pw[rows, :])
                vp[at, :] = vp[at, :] + total if far else total
                return carry

            lax.fori_loop(0, 4, conf_block, 0)

        def recv_half(far):
            def step(k, carry):
                frm = target(2 * k + far)
                send_p(c, 2 * k + far, frm, frm).wait_recv()
                return carry

            lax.fori_loop(1 - far, side, step, 0)

        own_p[c].wait()
        recv_half(0)
        conf_half(0)
        recv_half(1)
        conf_half(1)

        def deriv_block(i, carry):
            at = pl.ds(pl.multiple_of(i * half, half), half)
            for p in range(3):
                high, low = split(field(vp, p, at))
                dp[at, 2 * p * LANES : (2 * p + 2) * LANES] = dot3(high, low, both_h[...], both_l[...])
            return carry

        lax.fori_loop(0, 2, deriv_block, 0)

        def local_block(i, carry):
            at = pl.ds(pl.multiple_of(i * ROWS, ROWS), ROWS)
            dth_at = pl.ds(pl.multiple_of(PLANES + i * ROWS, ROWS), ROWS)
            u_r, u_t, u_z = [field(vv, f, at) for f in range(3)]
            spin = u_t * inv_r
            ur2, spin2, uz2 = [jnp.where(in_c, v, swap(v)) for v in (u_r, spin, u_z)]
            psi, advect = [], []
            for p in range(3):
                value = field(vp, p, at)
                other = swap(value)
                for h in range(2):
                    psi.append(jnp.where(in_c, value if h == c else other, 0.0))
                advect.append(
                    ur2 * field(dp, 2 * p, at) + spin2 * field(vp, p, dth_at) + uz2 * field(dp, 2 * p + 1, at)
                )
            conform, inverse = exponentials(psi)
            g = [field(proj, j, at) for j in range(9)]
            wa, wb, wc = 0.5 * (g[1] - g[3]), 0.5 * (g[2] - g[6]), 0.5 * (g[5] - g[7])
            wa2 = wa + spin
            r0 = [wa2 * psi[1] + wb * psi[2], wa2 * psi[3] + wb * psi[4], wa2 * psi[4] + wb * psi[5]]
            r1 = [wc * psi[2] - wa2 * psi[0], wc * psi[4] - wa2 * psi[1], wc * psi[5] - wa2 * psi[2]]
            r2 = [-(wb * psi[j] + wc * psi[k]) for j, k in ((0, 1), (1, 3), (2, 4))]
            rate = [
                2.0 * (r0[0] + g[0]),
                r0[1] + r1[0] + (g[1] + g[3]),
                r0[2] + r2[0] + (g[2] + g[6]),
                2.0 * (r1[1] + g[4]),
                r1[2] + r2[1] + (g[5] + g[7]),
                2.0 * (r2[2] + g[8]),
            ]
            for m in range(6):
                unit = 1.0 if m in diag else 0.0
                rate[m] = rate[m] - (1.0 / RELAX_TIME) * (
                    unit - inverse[m] + MOBILITY * (conform[m] - 2.0 * unit + inverse[m])
                )
            stress = [conform[m] - 1.0 if m in diag else conform[m] for m in range(6)]
            for f, (m, n) in enumerate(((0, 2), (1, 4), (2, 5))):
                high, low = split(pair_up(c, stress[m], stress[n]))
                sth[at, f * LANES : (f + 1) * LANES] = high
                stl[at, f * LANES : (f + 1) * LANES] = low
            hoop = [stress[m] * inv_r for m in (1, 3, 4)]
            base = [
                field(conv, 0, at) + (stress[0] - stress[3]) * inv_r,
                field(conv, 1, at) + 2.0 * hoop[0],
                field(conv, 2, at) + stress[2] * inv_r,
            ]
            mom[at, :LANES] = pair_up(c, base[0], base[1])
            mom[at, LANES:] = pair_up(c, base[2], rate[5]) - jnp.where(lo, 0.0, advect[2])
            put_rate(at, 2, pair_up(c, rate[0], rate[1]) - advect[0])
            put_rate(at, 3, pair_up(c, rate[2], rate[3]) - advect[1])
            first = rate[4] if c == 0 else swap(rate[4])
            put_rate(at, 4, jnp.where(lo, first - advect[2], 0.0))
            put_rate(at, 5, pair_up(c, hoop[0], hoop[1]))
            last = hoop[2] if c == 0 else swap(hoop[2])
            put_rate(at, 6, jnp.where(lo, last, 0.0))
            return carry

        lax.fori_loop(0, PLANES // ROWS, local_block, 0)
        if c == 0:
            loads[3].wait()

        def div_block(i, carry):
            at = pl.ds(pl.multiple_of(i * half, half), half)
            for f, cols in enumerate((slice(0, wide), slice(wide, 3 * LANES))):
                depth = cols.stop - cols.start
                total = dot3(
                    sth[at, cols], stl[at, cols], div_ref[:depth, :LANES], div_ref[:depth, LANES:]
                )
                put_rate(at, f, field(mom, f, at) + total)
            return carry

        lax.fori_loop(0, 2, div_block, 0)
        if c == 0:
            for load in loads[4:]:
                load.wait()

        def back_block(step, carry):
            pair = lax.rem(quarter // 2 + 1 + step // 2, 2)
            i = pair * 2 + lax.rem(quarter + step + step // 2, 2)
            at = pl.ds(pl.multiple_of(i * share, share), share)
            dst = pl.ds(i * per, per)
            cols, hoops = slice(0, wide), slice(5 * LANES, 7 * LANES)
            total = dot3(bh_ref[at, :PLANES], bl_ref[at, :PLANES], rh[:, cols], rl[:, cols])
            total += dot3(bh_ref[at, PLANES:], bl_ref[at, PLANES:], rh[:, hoops], rl[:, hoops])
            coefs = [total[:, :LANES], total[:, LANES:]]
            cols = slice(wide, 5 * LANES)
            total = dot3(bh_ref[at, :PLANES], bl_ref[at, :PLANES], rh[:, cols], rl[:, cols])
            coefs += [total[:, j * LANES : (j + 1) * LANES] for j in range(3)]
            if c == 0:
                blocks = [None] * 4
                for f in range(9):
                    off = f * KEPT
                    b, inside = off // LANES, off % LANES
                    moved = rolled(coefs[f // 2], inside - f % 2 * CELL)
                    blocks[b] = moved if inside == 0 else jnp.where(lane < inside, blocks[b], moved)
                    if inside + KEPT > LANES:
                        blocks[b + 1] = moved
                for p in range(4):
                    back0[dst, p] = blocks[p].reshape(per, modes, LANES)
                for p in range(5):
                    kept[p, at, :] = coefs[p]
            else:
                for p in range(5):
                    face = rolled(kept[p, at, :], NODE_1D - CELL)
                    coefs[p] = jnp.where(lane % CELL < NODE_1D, 0.5 * (coefs[p] + face), coefs[p])
                for p in range(5):
                    value = coefs[p].reshape(per, modes, LANES)
                    if not fold:
                        back1[dst, p] = value
                    elif p < 4:
                        back1[dst, 2 * p] = value[:, : modes // 2]
                        back1[dst, 2 * p + 1] = value[:, modes // 2 :]
                    else:
                        upper = swap(coefs[p]).reshape(per, modes, LANES)
                        back1[dst, 8] = jnp.where(lo[None], value[:, : modes // 2], upper[:, modes // 2 :])

            def give_start(j, inner):
                to = i * per + lax.rem(me + j, per)

                @pl.when(to != me)
                def _():
                    give(c, to, me).start()

                return inner

            lax.fori_loop(0, per, give_start, 0)
            return carry

        lax.fori_loop(0, 4, back_block, 0)

    cycle_part(0)
    cycle_part(1)
    own = [pltpu.make_async_copy(backs[c].at[me], outs[c].at[me], local_sem.at[c]) for c in range(2)]
    for copy in own:
        copy.start()
    every(lambda k, to: send_v(k, to, me).wait_send())
    for c in range(2):
        every(lambda k, to, c=c: send_p(c, k, to, me).wait_send())
    for copy in own:
        copy.wait()

    def give_wait(k, to):
        for c in range(2):
            give(c, to, to).wait_recv()
            give(c, to, me).wait_send()

    every(give_wait)


def final_kernel(
    n_dev, modes, fold, group,
    orient_ref, wall_ref, below0_ref, below1_ref, first_ref, second_ref, above0_ref, above1_ref, vel_ref, logc_ref,
    vel_out, logc_out,
):
    step = pl.program_id(0)
    me = lax.axis_index("mode")
    lane = lax.broadcasted_iota(jnp.int32, (1, LANES), 1)
    lo = lane < CELL
    top = lane % NODE_1D == NODE_1D - 1
    low_rows = lane % NODE_1D == 0
    grid = lax.broadcasted_iota(jnp.int32, (LANES, LANES), 0)
    stored = lax.broadcasted_iota(jnp.int32, (LANES, LANES), 1)
    mode_ids = me * modes + lax.broadcasted_iota(jnp.int32, (modes, 1), 0)
    speed = jnp.where(mode_ids == 0, wall_ref[0], 0.0)
    cycle = lane // CELL
    lead = lane // NODE_1D % NODE_1D
    trail = lane % NODE_1D

    def rolled(value, shift):
        return pltpu.roll(value, shift % LANES, 1) if shift % LANES else value

    def layer_fields(ref0, ref1, at):
        fields = []
        for f in range(9):
            off = f * KEPT
            b, inside = off // LANES, off % LANES
            zero = rolled(ref0[at, b], -inside)
            if inside + KEPT > LANES:
                zero = jnp.where(lane < LANES - inside, zero, rolled(ref0[at, b + 1], -inside))
            p = f // 2
            if not fold:
                one = rolled(ref1[at, p], (f + 1) % 2 * CELL)
            elif p < 4:
                one = ref1[at, 2 * p : 2 * p + 2].reshape(modes, LANES)
                one = rolled(one, (f + 1) % 2 * CELL)
            else:
                one = jnp.concatenate([rolled(ref1[at, 8], CELL), ref1[at, 8]], axis=0)
            fields.append(jnp.where(lo, zero, one))
        return fields

    layers = [layer_fields(below0_ref, below1_ref, 0)]
    layers += [layer_fields(first_ref, second_ref, g) for g in range(group)]
    layers.append(layer_fields(above0_ref, above1_ref, 0))
    for g in range(group):
        layer = step * group + g
        place = stored_index(orient_ref, layer, grid)
        twin = stored_index(orient_ref, layer, grid - NODE_1D)
        is_face = jnp.logical_and(grid >= CELL, grid < CELL + NODE_1D)
        dropped = jnp.logical_and(grid >= KEPT, grid < CELL)
        hit = jnp.logical_and(place == stored, jnp.logical_not(dropped))
        hit = jnp.logical_or(hit, jnp.logical_and(is_face, twin == stored))
        hot = jnp.where(hit, 1.0, 0.0).astype(BF)
        hot = jnp.concatenate([hot, hot], axis=0)
        code = jnp.zeros_like(lane)
        for c in range(CYCLES):
            code = jnp.where(cycle == c, orient_ref[layer * CYCLES + c], code)
        flipped_a = jnp.where(code % 2 == 1, NODE_1D - 1 - lead, lead)
        flipped_b = jnp.where(code // 2 % 2 == 1, NODE_1D - 1 - trail, trail)
        x = jnp.where(code // 4 % 2 == 1, flipped_a, flipped_b)
        inner = jnp.logical_and(cycle == 0, x == 0)
        outer = jnp.logical_and(cycle == CYCLES - 1, x == NODE_1D - 1)
        on_wall = jnp.logical_or(inner, outer)
        cols = slice(g * LANES, (g + 1) * LANES)
        many = 9 if modes % 8 == 0 else 1
        for start in range(0, 9, many):
            rates = []
            for c in range(start, start + many):
                f = SLOT_OF[c]
                below, rate, above = [layers[g + d][f] for d in range(3)]
                other = jnp.where(low_rows, rolled(below, 1 - NODE_1D), rolled(above, NODE_1D - 1))
                rates.append(jnp.where(jnp.logical_or(top, low_rows), 0.5 * (rate + other), rate))
            rate = jnp.concatenate(rates, axis=0) if many > 1 else rates[0]
            high, low = split(rate)
            rate = STEP_DT * dot(jnp.concatenate([high, low], axis=1), hot)
            for j in range(many):
                c = start + j
                own = rate[j * modes : (j + 1) * modes]
                if c < 3:
                    wall = jnp.where(inner, speed, 0.0) if c == 1 else 0.0
                    vel_out[c, :, cols] = jnp.where(on_wall, wall, vel_ref[c, :, cols] + own)
                else:
                    logc_out[c - 3, :, cols] = logc_ref[c - 3, :, cols] + own


def body(velocity, log_conf, orientation, wall_speed):
    n_dev = lax.axis_size("mode")
    modes = velocity.shape[1]
    fold = modes % 16 == 0
    tail = (9, modes // 2, LANES) if fold else (5, modes, LANES)
    consts = [jnp.asarray(t) for t in tables()]
    hbm = pl.BlockSpec(memory_space=pl.ANY)
    smem = pl.BlockSpec(memory_space=pltpu.SMEM)
    dma = pltpu.SemaphoreType.DMA
    face_rows = PLANES + PLANES * CYCLES * NODE_1D // LANES
    first, second = pl.pallas_call(
        functools.partial(main_kernel, n_dev, modes, fold),
        out_shape=(
            jax.ShapeDtypeStruct((n_dev, 4, modes, LANES), F32),
            jax.ShapeDtypeStruct((n_dev, *tail), F32),
        ),
        in_specs=[hbm, hbm, smem] + [hbm] * len(consts),
        out_specs=(hbm, hbm),
        scratch_shapes=[pltpu.VMEM(t.shape, t.dtype) for t in consts]
        + [
            pltpu.VMEM(log_conf.shape, F32),
            pltpu.VMEM((2, n_dev, 3, modes, LANES), F32),
            pltpu.VMEM((n_dev, 3, modes, LANES), F32),
            pltpu.VMEM((2, n_dev, 3, modes, LANES), F32),
            pltpu.VMEM((PLANES, 3 * LANES), BF),
            pltpu.VMEM((PLANES, 3 * LANES), BF),
            pltpu.VMEM((PLANES, 3 * LANES), BF),
            pltpu.VMEM((PLANES, 3 * LANES), BF),
            pltpu.VMEM((2 * PLANES, 3 * LANES), F32),
            pltpu.VMEM((2 * PLANES, 3 * LANES), F32),
            pltpu.VMEM((PLANES, 6 * LANES), F32),
            pltpu.VMEM((PLANES, 9 * LANES), F32),
            pltpu.VMEM((2, face_rows, LANES), F32),
            pltpu.VMEM((2, face_rows, LANES), F32),
            pltpu.VMEM((PLANES, 3 * LANES), F32),
            pltpu.VMEM((PLANES, 2 * LANES), F32),
            pltpu.VMEM((PLANES, 3 * LANES), BF),
            pltpu.VMEM((PLANES, 3 * LANES), BF),
            pltpu.VMEM((PLANES, 7 * LANES), BF),
            pltpu.VMEM((PLANES, 7 * LANES), BF),
            pltpu.VMEM((5, PLANES, LANES), F32),
            pltpu.VMEM((n_dev, 4, modes, LANES), F32),
            pltpu.VMEM((n_dev, *tail), F32),
            dma((4,)),
            dma((len(consts),)),
            dma((n_dev,)),
            dma((n_dev,)),
            dma((2, n_dev)),
            dma((2, n_dev)),
            dma((2,)),
            dma((2,)),
            dma((2, n_dev)),
            dma((2, n_dev)),
        ],
        compiler_params=pltpu.CompilerParams(
            collective_id=0, has_side_effects=True, vmem_limit_bytes=60 * 2**20
        ),
        name="fields",
    )(velocity, log_conf, orientation, *consts)

    group = 8
    tile = group * LANES

    def below_of(i):
        return (lax.rem(i * group + n_dev - 1, n_dev), 0, 0, 0)

    def above_of(i):
        return (lax.rem(i * group + group, n_dev), 0, 0, 0)

    def here(i):
        return (i, 0, 0, 0)

    return pl.pallas_call(
        functools.partial(final_kernel, n_dev, modes, fold, group),
        grid=(n_dev // group,),
        out_shape=(
            jax.ShapeDtypeStruct(velocity.shape, F32),
            jax.ShapeDtypeStruct(log_conf.shape, F32),
        ),
        in_specs=[
            smem,
            smem,
            pl.BlockSpec((1, 4, modes, LANES), below_of),
            pl.BlockSpec((1, *tail), below_of),
            pl.BlockSpec((group, 4, modes, LANES), here),
            pl.BlockSpec((group, *tail), here),
            pl.BlockSpec((1, 4, modes, LANES), above_of),
            pl.BlockSpec((1, *tail), above_of),
            pl.BlockSpec((3, modes, tile), lambda i: (0, 0, i)),
            pl.BlockSpec((6, modes, tile), lambda i: (0, 0, i)),
        ],
        out_specs=(
            pl.BlockSpec((3, modes, tile), lambda i: (0, 0, i)),
            pl.BlockSpec((6, modes, tile), lambda i: (0, 0, i)),
        ),
        compiler_params=pltpu.CompilerParams(vmem_limit_bytes=60 * 2**20),
        name="finish",
    )(orientation, wall_speed, first, second, first, second, first, second, velocity, log_conf)


def solution(mesh):
    in_specs = (P("ens", "mode", None), P("ens", "mode", None), P(), P("ens"))
    out_specs = (P("ens", "mode", None), P("ens", "mode", None))
    return jax.shard_map(body, mesh=mesh, in_specs=in_specs, out_specs=out_specs, check_vma=False)
```

time: 128 us -> 121 us (0.945)
  Pallas kernels: 126 us -> 119 us
    pallas_call x2, Pallas kernels: 126 us -> 119 us  [the longest x1 113 us: body(): pl.pallas_call(functools.partial(main_kernel, n_dev, modes, fold), out_sh...]
where the time goes in v1:
time: 121 us
  Pallas kernels  119 us (98%)
  between operations  1.28 us (1%)
    pallas_call x1, Pallas kernels, body(): pl.pallas_call(functools.partial(main_kernel, n_dev, modes, fold), out_sh...  113 us
    pallas_call x1, Pallas kernels, body(): pl.pallas_call(functools.partial(final_kernel, n_dev, modes, fold, group)...  5.9 us

profile of v1, /device:TPU:15, one launch (start us, length us, event | category | flops | bytes accessed | tf_op | source)
XLA Modules:
  0.0 120.7 jit_solution(8246469334133701989)
XLA Ops:
  1.3 113.5 %fields.1 = (f32[16,4,32,128]{3,2,1,0:T(8,128)}, f32[16,9,16,128]{3,2,1,0:T(8,128)}) custom-call(f32[3,32,2048]{2,1,0:T(8,128)} %vel_ref.3, f32[6,32,2048]{2,1,0:T(8,128)} %logc_ref.3, s32[32]{0:T(128)} %orient_ref.3, bf16[1024,512]{1,0:T(8,128)(2,1)} %constant.12.clone.fh_in, bf16[1024,512]{1,0:T(8,128)(2,1)} %constant.13.clone.fl_in, ...), custom_call_target="tpu_custom_call" | custom-call | tf_op jit(solution)/shard_map/fields/pallas_call | solution.py:703
  114.8 5.9 %finish.1 = (f32[3,32,2048]{2,1,0:T(8,128)}, f32[6,32,2048]{2,1,0:T(8,128)}) custom-call(s32[32]{0:T(128)} %orient_ref.3, f32[1]{0:T(128)S(6)} %copy.12.wall_ref, f32[16,4,32,128]{3,2,1,0:T(8,128)} %get-tuple-element.4.below0_ref.first_ref.above0_ref, f32[16,9,16,128]{3,2,1,0:T(8,128)} %get-tuple-element.5.below1_ref.second_ref.above1_ref, ...), custom_call_target="tpu_custom_call" | custom-call | tf_op jit(solution)/shard_map/finish/pallas_call | solution.py:765

commit v2 on v1

--- a/solution.py
+++ b/solution.py
@@ -15,6 +15,7 @@
 CELL = NODE_1D * NODE_1D
 LANES = CYCLES * CELL
 KEPT = CELL - NODE_1D
+INSIDE = LANES - LANES // 4
 SLOT_OF = (0, 1, 2, 4, 5, 6, 7, 8, 3)
 STEP_DT = 0.002
 RELAX_TIME = 0.02
@@ -170,6 +171,12 @@
     return plus, minus
 
 
+def first_cycle(f):
+    wall = NODE_1D if f < 3 else 0
+    start = f * KEPT - min(f, 3) * NODE_1D
+    return start // LANES, start % LANES, wall, KEPT - wall
+
+
 def field(ref, f, rows=slice(None)):
     return ref[rows, f * LANES : (f + 1) * LANES]
 
@@ -278,8 +285,7 @@
         own_p[c].start()
 
     stored = lax.broadcasted_iota(jnp.int32, (LANES, LANES), 0)
-    grid = lax.broadcasted_iota(jnp.int32, (LANES, LANES), 1)
-    to_grid = jnp.where(stored_index(orient_ref, me, grid) == stored, 1.0, 0.0).astype(BF)
+    to_grid = jnp.where(stored_index(orient_ref, me, lane) == stored, 1.0, 0.0).astype(BF)
 
     half = PLANES // 2
     inv_r = inverse_radius(lane)
@@ -409,12 +415,14 @@
             device_id_type=MESH,
         )
 
+    def quarters(value):
+        return value.reshape(per, 4, modes // 4, LANES)
+
     def cycle_part(c):
         in_c = lo if c == 0 else jnp.logical_not(lo)
         o = orient_ref[me * CYCLES + c]
-        same = stored // CELL == grid // CELL
-        hit = jnp.logical_and(stored_of_grid(o, grid) == stored % CELL, same)
-        cell_grid = jnp.where(hit, 1.0, 0.0).astype(BF)
+        place = stored_of_grid(o, lane) + lane // CELL * CELL
+        cell_grid = jnp.where(place == stored, 1.0, 0.0).astype(BF)
 
         def conf_half(far):
             which = lax.rem(half_of + far, 2)
@@ -547,14 +555,21 @@
             if c == 0:
                 blocks = [None] * 4
                 for f in range(9):
-                    off = f * KEPT
-                    b, inside = off // LANES, off % LANES
-                    moved = rolled(coefs[f // 2], inside - f % 2 * CELL)
+                    b, inside, wall, width = first_cycle(f)
+                    moved = rolled(coefs[f // 2], inside - wall - f % 2 * CELL)
                     blocks[b] = moved if inside == 0 else jnp.where(lane < inside, blocks[b], moved)
-                    if inside + KEPT > LANES:
+                    if inside + width > LANES:
                         blocks[b + 1] = moved
                 for p in range(4):
-                    back0[dst, p] = blocks[p].reshape(per, modes, LANES)
+                    if not fold:
+                        back0[dst, p] = blocks[p].reshape(per, modes, LANES)
+                    elif p < 3:
+                        back0[dst, 4 * p : 4 * p + 4] = quarters(blocks[p])
+                    else:
+                        value = quarters(blocks[p])
+                        for j in range(3):
+                            extra = quarters(rolled(blocks[p], INSIDE - j * (LANES // 4)))[:, 3]
+                            back0[dst, 12 + j] = jnp.where(lane < INSIDE, value[:, j], extra)
                 for p in range(5):
                     kept[p, at, :] = coefs[p]
             else:
@@ -562,15 +577,14 @@
                     face = rolled(kept[p, at, :], NODE_1D - CELL)
                     coefs[p] = jnp.where(lane % CELL < NODE_1D, 0.5 * (coefs[p] + face), coefs[p])
                 for p in range(5):
-                    value = coefs[p].reshape(per, modes, LANES)
                     if not fold:
-                        back1[dst, p] = value
+                        back1[dst, p] = coefs[p].reshape(per, modes, LANES)
                     elif p < 4:
-                        back1[dst, 2 * p] = value[:, : modes // 2]
-                        back1[dst, 2 * p + 1] = value[:, modes // 2 :]
+                        back1[dst, 4 * p : 4 * p + 4] = quarters(coefs[p])
                     else:
-                        upper = swap(coefs[p]).reshape(per, modes, LANES)
-                        back1[dst, 8] = jnp.where(lo[None], value[:, : modes // 2], upper[:, modes // 2 :])
+                        value, upper = quarters(coefs[p]), quarters(swap(coefs[p]))
+                        for j in range(2):
+                            back1[dst, 16 + j] = jnp.where(lo, value[:, j], upper[:, 2 + j])
 
             def give_start(j, inner):
                 to = i * per + lax.rem(me + j, per)
@@ -607,7 +621,7 @@
 
 def final_kernel(
     n_dev, modes, fold, group,
-    orient_ref, wall_ref, below0_ref, below1_ref, first_ref, second_ref, above0_ref, above1_ref, vel_ref, logc_ref,
+    orient_ref, wall_ref, first_ref, second_ref, vel_ref, logc_ref,
     vel_out, logc_out,
 ):
     step = pl.program_id(0)
@@ -616,8 +630,9 @@
     lo = lane < CELL
     top = lane % NODE_1D == NODE_1D - 1
     low_rows = lane % NODE_1D == 0
-    grid = lax.broadcasted_iota(jnp.int32, (LANES, LANES), 0)
-    stored = lax.broadcasted_iota(jnp.int32, (LANES, LANES), 1)
+    stored = lax.broadcasted_iota(jnp.int32, (LANES, LANES), 0)
+    is_face = jnp.logical_and(lane >= CELL, lane < CELL + NODE_1D)
+    dropped = jnp.logical_and(lane >= KEPT, lane < CELL)
     mode_ids = me * modes + lax.broadcasted_iota(jnp.int32, (modes, 1), 0)
     speed = jnp.where(mode_ids == 0, wall_ref[0], 0.0)
     cycle = lane // CELL
@@ -627,38 +642,43 @@
     def rolled(value, shift):
         return pltpu.roll(value, shift % LANES, 1) if shift % LANES else value
 
-    def layer_fields(ref0, ref1, at):
+    def layer_fields(g):
+        at = lax.rem(step * group + g + n_dev, n_dev)
+        ref0, ref1 = first_ref, second_ref
         fields = []
+        blocks = [ref0[at, p] if not fold else ref0[at, 4 * p : 4 * p + 4].reshape(modes, LANES) for p in range(3)]
+        if not fold:
+            blocks.append(ref0[at, 3])
+        else:
+            units = [ref0[at, 12 + j] for j in range(3)]
+            piece = lane // (LANES // 4)
+            outer = [rolled(units[j], (j + 1) * (LANES // 4)) for j in range(3)]
+            units.append(jnp.where(piece == 0, outer[0], jnp.where(piece == 1, outer[1], outer[2])))
+            blocks.append(jnp.concatenate(units, axis=0))
         for f in range(9):
-            off = f * KEPT
-            b, inside = off // LANES, off % LANES
-            zero = rolled(ref0[at, b], -inside)
-            if inside + KEPT > LANES:
-                zero = jnp.where(lane < LANES - inside, zero, rolled(ref0[at, b + 1], -inside))
+            b, inside, wall, width = first_cycle(f)
+            zero = rolled(blocks[b], wall - inside)
+            if inside + width > LANES:
+                zero = jnp.where(lane < wall + LANES - inside, zero, rolled(blocks[b + 1], wall - inside))
             p = f // 2
             if not fold:
                 one = rolled(ref1[at, p], (f + 1) % 2 * CELL)
             elif p < 4:
-                one = ref1[at, 2 * p : 2 * p + 2].reshape(modes, LANES)
+                one = ref1[at, 4 * p : 4 * p + 4].reshape(modes, LANES)
                 one = rolled(one, (f + 1) % 2 * CELL)
             else:
-                one = jnp.concatenate([rolled(ref1[at, 8], CELL), ref1[at, 8]], axis=0)
+                one = ref1[at, 16:18].reshape(modes // 2, LANES)
+                one = jnp.concatenate([rolled(one, CELL), one], axis=0)
             fields.append(jnp.where(lo, zero, one))
         return fields
 
-    layers = [layer_fields(below0_ref, below1_ref, 0)]
-    layers += [layer_fields(first_ref, second_ref, g) for g in range(group)]
-    layers.append(layer_fields(above0_ref, above1_ref, 0))
+    layers = [layer_fields(g) for g in range(-1, group + 1)]
     for g in range(group):
         layer = step * group + g
-        place = stored_index(orient_ref, layer, grid)
-        twin = stored_index(orient_ref, layer, grid - NODE_1D)
-        is_face = jnp.logical_and(grid >= CELL, grid < CELL + NODE_1D)
-        dropped = jnp.logical_and(grid >= KEPT, grid < CELL)
-        hit = jnp.logical_and(place == stored, jnp.logical_not(dropped))
-        hit = jnp.logical_or(hit, jnp.logical_and(is_face, twin == stored))
-        hot = jnp.where(hit, 1.0, 0.0).astype(BF)
-        hot = jnp.concatenate([hot, hot], axis=0)
+        place = jnp.where(dropped, -1, stored_index(orient_ref, layer, lane))
+        twin = jnp.where(is_face, stored_index(orient_ref, layer, lane - NODE_1D), -1)
+        hot = jnp.where(jnp.logical_or(place == stored, twin == stored), 1.0, 0.0).astype(BF)
+        hot = jnp.concatenate([hot, hot], axis=1)
         code = jnp.zeros_like(lane)
         for c in range(CYCLES):
             code = jnp.where(cycle == c, orient_ref[layer * CYCLES + c], code)
@@ -669,6 +689,7 @@
         outer = jnp.logical_and(cycle == CYCLES - 1, x == NODE_1D - 1)
         on_wall = jnp.logical_or(inner, outer)
         cols = slice(g * LANES, (g + 1) * LANES)
+        held = pl.ds(pl.multiple_of(layer * LANES, LANES), LANES)
         many = 9 if modes % 8 == 0 else 1
         for start in range(0, 9, many):
             rates = []
@@ -679,35 +700,42 @@
                 rates.append(jnp.where(jnp.logical_or(top, low_rows), 0.5 * (rate + other), rate))
             rate = jnp.concatenate(rates, axis=0) if many > 1 else rates[0]
             high, low = split(rate)
-            rate = STEP_DT * dot(jnp.concatenate([high, low], axis=1), hot)
+            rate = STEP_DT * lax.dot_general(
+                jnp.concatenate([high, low], axis=1),
+                hot,
+                (((1,), (1,)), ((), ())),
+                preferred_element_type=F32,
+            )
             for j in range(many):
                 c = start + j
                 own = rate[j * modes : (j + 1) * modes]
                 if c < 3:
                     wall = jnp.where(inner, speed, 0.0) if c == 1 else 0.0
-                    vel_out[c, :, cols] = jnp.where(on_wall, wall, vel_ref[c, :, cols] + own)
+                    vel_out[c, :, cols] = jnp.where(on_wall, wall, vel_ref[c, :, held] + own)
                 else:
-                    logc_out[c - 3, :, cols] = logc_ref[c - 3, :, cols] + own
+                    logc_out[c - 3, :, cols] = logc_ref[c - 3, :, held] + own
 
 
 def body(velocity, log_conf, orientation, wall_speed):
     n_dev = lax.axis_size("mode")
     modes = velocity.shape[1]
-    fold = modes % 16 == 0
-    tail = (9, modes // 2, LANES) if fold else (5, modes, LANES)
+    fold = modes % 32 == 0
+    head = (15, modes // 4, LANES) if fold else (4, modes, LANES)
+    tail = (18, modes // 4, LANES) if fold else (5, modes, LANES)
     consts = [jnp.asarray(t) for t in tables()]
-    hbm = pl.BlockSpec(memory_space=pl.ANY)
+    hbm = pl.BlockSpec(memory_space=pltpu.HBM)
+    free = pl.BlockSpec(memory_space=pl.ANY)
     smem = pl.BlockSpec(memory_space=pltpu.SMEM)
     dma = pltpu.SemaphoreType.DMA
     face_rows = PLANES + PLANES * CYCLES * NODE_1D // LANES
     first, second = pl.pallas_call(
         functools.partial(main_kernel, n_dev, modes, fold),
         out_shape=(
-            jax.ShapeDtypeStruct((n_dev, 4, modes, LANES), F32),
+            jax.ShapeDtypeStruct((n_dev, *head), F32),
             jax.ShapeDtypeStruct((n_dev, *tail), F32),
         ),
         in_specs=[hbm, hbm, smem] + [hbm] * len(consts),
-        out_specs=(hbm, hbm),
+        out_specs=(free, free),
         scratch_shapes=[pltpu.VMEM(t.shape, t.dtype) for t in consts]
         + [
             pltpu.VMEM(log_conf.shape, F32),
@@ -731,7 +759,7 @@
             pltpu.VMEM((PLANES, 7 * LANES), BF),
             pltpu.VMEM((PLANES, 7 * LANES), BF),
             pltpu.VMEM((5, PLANES, LANES), F32),
-            pltpu.VMEM((n_dev, 4, modes, LANES), F32),
+            pltpu.VMEM((n_dev, *head), F32),
             pltpu.VMEM((n_dev, *tail), F32),
             dma((4,)),
             dma((len(consts),)),
@@ -745,23 +773,15 @@
             dma((2, n_dev)),
         ],
         compiler_params=pltpu.CompilerParams(
-            collective_id=0, has_side_effects=True, vmem_limit_bytes=60 * 2**20
+            collective_id=0, has_side_effects=True, vmem_limit_bytes=36 * 2**20
         ),
         name="fields",
-    )(velocity, log_conf, orientation, *consts)
+    )(*[pltpu.with_memory_space_constraint(v, pltpu.HBM) for v in (velocity, log_conf, orientation, *consts)])
 
     group = 8
     tile = group * LANES
 
-    def below_of(i):
-        return (lax.rem(i * group + n_dev - 1, n_dev), 0, 0, 0)
-
-    def above_of(i):
-        return (lax.rem(i * group + group, n_dev), 0, 0, 0)
-
-    def here(i):
-        return (i, 0, 0, 0)
-
+    vmem = pl.BlockSpec(memory_space=pltpu.VMEM)
     return pl.pallas_call(
         functools.partial(final_kernel, n_dev, modes, fold, group),
         grid=(n_dev // group,),
@@ -772,22 +792,18 @@
         in_specs=[
             smem,
             smem,
-            pl.BlockSpec((1, 4, modes, LANES), below_of),
-            pl.BlockSpec((1, *tail), below_of),
-            pl.BlockSpec((group, 4, modes, LANES), here),
-            pl.BlockSpec((group, *tail), here),
-            pl.BlockSpec((1, 4, modes, LANES), above_of),
-            pl.BlockSpec((1, *tail), above_of),
-            pl.BlockSpec((3, modes, tile), lambda i: (0, 0, i)),
-            pl.BlockSpec((6, modes, tile), lambda i: (0, 0, i)),
+            vmem,
+            vmem,
+            vmem,
+            vmem,
         ],
         out_specs=(
             pl.BlockSpec((3, modes, tile), lambda i: (0, 0, i)),
             pl.BlockSpec((6, modes, tile), lambda i: (0, 0, i)),
         ),
-        compiler_params=pltpu.CompilerParams(vmem_limit_bytes=60 * 2**20),
+        compiler_params=pltpu.CompilerParams(vmem_limit_bytes=24 * 2**20),
         name="finish",
-    )(orientation, wall_speed, first, second, first, second, first, second, velocity, log_conf)
+    )(pltpu.with_memory_space_constraint(orientation, pltpu.HBM), wall_speed, first, second, velocity, log_conf)
 
 
 def solution(mesh):

time: 121 us -> 119 us (0.983)
  Pallas kernels: 119 us -> 117 us
    pallas_call x1, Pallas kernels: 113 us -> 112 us  [body(): pl.pallas_call(functools.partial(main_kernel, n_dev, modes, fold), out_sh...]
where the time goes in v2:
time: 119 us; the launch traced here: 118 us
  Pallas kernels  117 us (98%)
  between operations  1.32 us (1%)
    pallas_call x1, Pallas kernels, body(): pl.pallas_call(functools.partial(main_kernel, n_dev, modes, fold), out_sh...  112 us
    pallas_call x1, Pallas kernels, body(): pl.pallas_call(functools.partial(final_kernel, n_dev, modes, fold, group)...  4.89 us

profile of v2, /device:TPU:15, one launch (start us, length us, event | category | flops | bytes accessed | tf_op | source)
XLA Modules:
  0.0 118.4 jit_solution(14545766986545155096)
XLA Ops:
  1.3 0.0 copy-start
  1.3 0.0 copy-start.1
  1.3 112.2 %fields.1 = (f32[16,15,8,128]{3,2,1,0:T(8,128)S(1)}, f32[16,18,8,128]{3,2,1,0:T(8,128)S(1)}) custom-call(f32[3,32,2048]{2,1,0:T(8,128)} %vel_ref.3, f32[6,32,2048]{2,1,0:T(8,128)} %logc_ref.3, s32[32]{0:T(128)} %orient_ref.3, bf16[1024,512]{1,0:T(8,128)(2,1)} %constant.12.clone.fh_in, bf16[1024,512]{1,0:T(8,128)(2,1)} %constant.13.clone.fl_in, ...), custom_call_target="tpu_custom_call" | custom-call | tf_op jit(solution)/shard_map/fields/pallas_call | solution.py:731
  113.5 0.0 copy-done
  113.5 0.0 copy-done.1
  113.5 4.9 %finish.1 = (f32[3,32,2048]{2,1,0:T(8,128)}, f32[6,32,2048]{2,1,0:T(8,128)}) custom-call(s32[32]{0:T(128)} %orient_ref.3, f32[1]{0:T(128)S(6)} %copy.12.wall_ref, f32[16,15,8,128]{3,2,1,0:T(8,128)S(1)} %get-tuple-element.4.first_ref, f32[16,18,8,128]{3,2,1,0:T(8,128)S(1)} %get-tuple-element.5.second_ref, f32[3,32,2048]{2,1,0:T(8,128)S(1)} %copy-done.1, ...), custom_call_target="tpu_custom_call" | custom-call | tf_op jit(solution)/shard_map/finish/pallas_call | solution.py:785
Async XLA Ops:
  1.3 112.2 %copy-start = (f32[6,32,2048]{2,1,0:T(8,128)S(1)}, f32[6,32,2048]{2,1,0:T(8,128)}, u32[]{:S(2)}) copy-start(f32[6,32,2048]{2,1,0:T(8,128)} %logc_ref.3) | copy-start | bytes 4718596
  1.3 112.2 %copy-start.1 = (f32[3,32,2048]{2,1,0:T(8,128)S(1)}, f32[3,32,2048]{2,1,0:T(8,128)}, u32[]{:S(2)}) copy-start(f32[3,32,2048]{2,1,0:T(8,128)} %vel_ref.3) | copy-start | bytes 2359300

commit v3 on v2

--- a/solution.py
+++ b/solution.py
@@ -16,7 +16,7 @@
 LANES = CYCLES * CELL
 KEPT = CELL - NODE_1D
 INSIDE = LANES - LANES // 4
-SLOT_OF = (0, 1, 2, 4, 5, 6, 7, 8, 3)
+CHANNEL_OF = (0, 1, 2, 8, 3, 4, 5, 6, 7)
 STEP_DT = 0.002
 RELAX_TIME = 0.02
 MOBILITY = 0.3
@@ -281,7 +281,8 @@
             return carry
 
         lax.fori_loop(0, n_dev, pack_psi, 0)
-        every(lambda k, to, c=c: send_p(c, k, to, me).start())
+        if c == 0:
+            every(lambda k, to: send_p(0, k, to, me).start())
         own_p[c].start()
 
     stored = lax.broadcasted_iota(jnp.int32, (LANES, LANES), 0)
@@ -295,20 +296,32 @@
     both_h, both_l, grad_h, grad_l = [node_ref.at[:, i * wide : (i + 1) * wide] for i in range(4)]
     mean_ref = node_ref.at[:, 4 * wide : 4 * wide + LANES]
 
+    def vel_half(far):
+        def step(k, carry):
+            frm = target(2 * k + far)
+            send_v(2 * k + far, frm, frm).wait_recv()
+            return carry
+
+        lax.fori_loop(1 - far, side, step, 0)
+        which = lax.rem(half_of + far, 2)
+        rows = pl.ds(pl.multiple_of(which * half, half), half)
+        for f in range(3):
+            high, low = split(xv[pl.ds(which * side, side), f].reshape(half, LANES))
+            at = slice(f * LANES, (f + 1) * LANES)
+            xh[rows, at] = dot(high, to_grid).astype(BF)
+            xl[rows, at] = dot(low, to_grid).astype(BF)
+
+        def velocity_block(i, carry):
+            at = pl.ds(pl.multiple_of(i * half, half), half)
+            total = dot3(fh_ref[at, rows], fl_ref[at, rows], xh[rows, :], xl[rows, :])
+            vv[at, :] = vv[at, :] + total if far else total
+            return carry
+
+        lax.fori_loop(0, 4, velocity_block, 0)
+
     own_v.wait()
-    every(lambda k, frm: send_v(k, frm, frm).wait_recv())
-    for f in range(3):
-        high, low = split(xv[:, f].reshape(PLANES, LANES))
-        at = slice(f * LANES, (f + 1) * LANES)
-        xh[:, at] = dot(high, to_grid).astype(BF)
-        xl[:, at] = dot(low, to_grid).astype(BF)
-
-    def velocity_block(i, carry):
-        at = pl.ds(pl.multiple_of(i * half, half), half)
-        vv[at, :] = dot3(fh_ref[at, :], fl_ref[at, :], xh[...], xl[...])
-        return carry
-
-    lax.fori_loop(0, 4, velocity_block, 0)
+    vel_half(0)
+    vel_half(1)
 
     def grad_block(i, carry):
         block = half // 2
@@ -366,6 +379,7 @@
 
     for face in faces:
         face.wait()
+    every(lambda k, to: send_p(1, k, to, me).start())
 
     top = lane % NODE_1D == NODE_1D - 1
     low_rows = lane % NODE_1D == 0
@@ -631,8 +645,9 @@
     top = lane % NODE_1D == NODE_1D - 1
     low_rows = lane % NODE_1D == 0
     stored = lax.broadcasted_iota(jnp.int32, (LANES, LANES), 0)
-    is_face = jnp.logical_and(lane >= CELL, lane < CELL + NODE_1D)
-    dropped = jnp.logical_and(lane >= KEPT, lane < CELL)
+    edge = jnp.logical_or(top, low_rows)
+    jump = jnp.where(low_rows, NODE_1D - 1, jnp.where(top, 1 - NODE_1D, 0))
+    weight = jnp.where(edge, 0.5 * STEP_DT, STEP_DT)
     mode_ids = me * modes + lax.broadcasted_iota(jnp.int32, (modes, 1), 0)
     speed = jnp.where(mode_ids == 0, wall_ref[0], 0.0)
     cycle = lane // CELL
@@ -657,28 +672,37 @@
             blocks.append(jnp.concatenate(units, axis=0))
         for f in range(9):
             b, inside, wall, width = first_cycle(f)
-            zero = rolled(blocks[b], wall - inside)
+            shift = wall - inside + (f + 1) % 2 * CELL
+            zero = rolled(blocks[b], shift)
             if inside + width > LANES:
-                zero = jnp.where(lane < wall + LANES - inside, zero, rolled(blocks[b + 1], wall - inside))
+                zero = jnp.where(lane < shift + LANES, zero, rolled(blocks[b + 1], shift))
             p = f // 2
             if not fold:
-                one = rolled(ref1[at, p], (f + 1) % 2 * CELL)
+                one = ref1[at, p]
             elif p < 4:
                 one = ref1[at, 4 * p : 4 * p + 4].reshape(modes, LANES)
-                one = rolled(one, (f + 1) % 2 * CELL)
             else:
                 one = ref1[at, 16:18].reshape(modes // 2, LANES)
-                one = jnp.concatenate([rolled(one, CELL), one], axis=0)
-            fields.append(jnp.where(lo, zero, one))
+                one = jnp.concatenate([one, rolled(one, CELL)], axis=0)
+            fields.append(jnp.where(lo, zero, one) if f % 2 else jnp.where(lo, one, zero))
         return fields
 
     layers = [layer_fields(g) for g in range(-1, group + 1)]
     for g in range(group):
         layer = step * group + g
-        place = jnp.where(dropped, -1, stored_index(orient_ref, layer, lane))
-        twin = jnp.where(is_face, stored_index(orient_ref, layer, lane - NODE_1D), -1)
-        hot = jnp.where(jnp.logical_or(place == stored, twin == stored), 1.0, 0.0).astype(BF)
-        hot = jnp.concatenate([hot, hot], axis=1)
+        hots = []
+        for nat in ((lane + CELL) % LANES, lane):
+            parts = []
+            for to in (nat, nat + jump):
+                here = jnp.logical_or(nat < KEPT, nat >= CELL)
+                face = jnp.logical_and(nat >= CELL, nat < CELL + NODE_1D)
+                if parts:
+                    here, face = jnp.logical_and(here, edge), jnp.logical_and(face, edge)
+                place = jnp.where(here, stored_index(orient_ref, layer, to), -1)
+                twin = jnp.where(face, stored_index(orient_ref, layer, to - NODE_1D), -1)
+                hit = jnp.logical_or(place == stored, twin == stored)
+                parts += [jnp.where(hit, 1.0, 0.0).astype(BF)] * 2
+            hots.append(jnp.concatenate(parts, axis=1))
         code = jnp.zeros_like(lane)
         for c in range(CYCLES):
             code = jnp.where(cycle == c, orient_ref[layer * CYCLES + c], code)
@@ -690,25 +714,25 @@
         on_wall = jnp.logical_or(inner, outer)
         cols = slice(g * LANES, (g + 1) * LANES)
         held = pl.ds(pl.multiple_of(layer * LANES, LANES), LANES)
-        many = 9 if modes % 8 == 0 else 1
-        for start in range(0, 9, many):
-            rates = []
-            for c in range(start, start + many):
-                f = SLOT_OF[c]
+        many = modes % 8 == 0
+        for fields in ((0, 2, 4, 6, 8), (1, 3, 5, 7)) if many else [(f,) for f in range(9)]:
+            rates, others = [], []
+            for f in fields:
                 below, rate, above = [layers[g + d][f] for d in range(3)]
-                other = jnp.where(low_rows, rolled(below, 1 - NODE_1D), rolled(above, NODE_1D - 1))
-                rates.append(jnp.where(jnp.logical_or(top, low_rows), 0.5 * (rate + other), rate))
-            rate = jnp.concatenate(rates, axis=0) if many > 1 else rates[0]
-            high, low = split(rate)
-            rate = STEP_DT * lax.dot_general(
-                jnp.concatenate([high, low], axis=1),
-                hot,
+                rates.append(weight * rate)
+                others.append((0.5 * STEP_DT) * jnp.where(top, below, above))
+            pieces = []
+            for part in (rates, others):
+                pieces += split(jnp.concatenate(part, axis=0) if many else part[0])
+            total = lax.dot_general(
+                jnp.concatenate(pieces, axis=1),
+                hots[fields[0] % 2],
                 (((1,), (1,)), ((), ())),
                 preferred_element_type=F32,
             )
-            for j in range(many):
-                c = start + j
-                own = rate[j * modes : (j + 1) * modes]
+            for j, f in enumerate(fields):
+                c = CHANNEL_OF[f]
+                own = total[j * modes : (j + 1) * modes]
                 if c < 3:
                     wall = jnp.where(inner, speed, 0.0) if c == 1 else 0.0
                     vel_out[c, :, cols] = jnp.where(on_wall, wall, vel_ref[c, :, held] + own)

time: 119 us -> 116 us (0.975)
  Pallas kernels: 117 us -> 115 us
    pallas_call x1, Pallas kernels: 112 us -> 110 us  [body(): pl.pallas_call(functools.partial(main_kernel, n_dev, modes, fold), out_sh...]
where the time goes in v3:
time: 116 us
  Pallas kernels  115 us (99%)
  between operations  1.32 us (1%)
    pallas_call x1, Pallas kernels, body(): pl.pallas_call(functools.partial(main_kernel, n_dev, modes, fold), out_sh...  110 us
    pallas_call x1, Pallas kernels, body(): pl.pallas_call(functools.partial(final_kernel, n_dev, modes, fold, group)...  4.59 us

profile of v3, /device:TPU:15, one launch (start us, length us, event | category | flops | bytes accessed | tf_op | source)
XLA Modules:
  0.0 115.8 jit_solution(1305090220101985981)
XLA Ops:
  1.3 0.0 copy-start
  1.3 0.0 copy-start.1
  1.3 109.9 %fields.1 = (f32[16,15,8,128]{3,2,1,0:T(8,128)S(1)}, f32[16,18,8,128]{3,2,1,0:T(8,128)S(1)}) custom-call(f32[3,32,2048]{2,1,0:T(8,128)} %vel_ref.3, f32[6,32,2048]{2,1,0:T(8,128)} %logc_ref.3, s32[32]{0:T(128)} %orient_ref.3, bf16[1024,512]{1,0:T(8,128)(2,1)} %constant.12.clone.fh_in, bf16[1024,512]{1,0:T(8,128)(2,1)} %constant.13.clone.fl_in, ...), custom_call_target="tpu_custom_call" | custom-call | tf_op jit(solution)/shard_map/fields/pallas_call | solution.py:755
  111.2 0.0 copy-done
  111.2 0.0 copy-done.1
  111.3 4.6 %finish.1 = (f32[3,32,2048]{2,1,0:T(8,128)}, f32[6,32,2048]{2,1,0:T(8,128)}) custom-call(s32[32]{0:T(128)} %orient_ref.3, f32[1]{0:T(128)S(6)} %copy.12.wall_ref, f32[16,15,8,128]{3,2,1,0:T(8,128)S(1)} %get-tuple-element.4.first_ref, f32[16,18,8,128]{3,2,1,0:T(8,128)S(1)} %get-tuple-element.5.second_ref, f32[3,32,2048]{2,1,0:T(8,128)S(1)} %copy-done.1, ...), custom_call_target="tpu_custom_call" | custom-call | tf_op jit(solution)/shard_map/finish/pallas_call | solution.py:809
Async XLA Ops:
  1.3 110.0 %copy-start = (f32[6,32,2048]{2,1,0:T(8,128)S(1)}, f32[6,32,2048]{2,1,0:T(8,128)}, u32[]{:S(2)}) copy-start(f32[6,32,2048]{2,1,0:T(8,128)} %logc_ref.3) | copy-start | bytes 4718596
  1.3 110.0 %copy-start.1 = (f32[3,32,2048]{2,1,0:T(8,128)S(1)}, f32[3,32,2048]{2,1,0:T(8,128)}, u32[]{:S(2)}) copy-start(f32[3,32,2048]{2,1,0:T(8,128)} %vel_ref.3) | copy-start | bytes 2359300

commit v4 on v3

--- a/solution.py
+++ b/solution.py
@@ -183,10 +183,10 @@
 
 def main_kernel(
     n_dev, modes, fold,
-    vel_ref, logc_ref, orient_ref, fh_in, fl_in, bh_in, bl_in, node_in, div_in,
-    out0_ref, out1_ref,
+    vel_ref, logc_ref, orient_in, wall_ref, fh_in, fl_in, bh_in, bl_in, node_in, div_in,
+    vel_out, logc_out,
     fh_ref, fl_ref, bh_ref, bl_ref, node_ref, div_ref,
-    raw, packed, xv, xp, xh, xl, ph, pw, vv, vp, dp, proj, face_out, face_in, conv, mom, sth, stl, rh, rl,
+    orient_ref, out0_ref, out1_ref, packed, xv, xp, xh, xl, ph, pw, vv, vp, dp, proj, face_out, face_in, conv, mom, sth, stl, rh, rl,
     kept, back0, back1,
     local_sem, const_sem, vs_sem, vr_sem, ps_sem, pr_sem, fs_sem, fr_sem, bs_sem, br_sem,
 ):
@@ -203,8 +203,12 @@
         return carry
 
     lax.fori_loop(1, n_dev, greet, 0)
-    load_logc = pltpu.make_async_copy(logc_ref, raw, local_sem.at[0])
-    load_logc.start()
+    early = [
+        pltpu.make_async_copy(a, b, local_sem.at[i])
+        for i, (a, b) in ((0, (logc_ref, logc_out)), (4, (orient_in, orient_ref)))
+    ]
+    for copy in early:
+        copy.start()
     pl.semaphore_wait(barrier, n_dev - 1)
 
     side = n_dev // 2
@@ -247,6 +251,8 @@
     every(lambda k, to: send_v(k, to, me).start())
     own_v = pltpu.make_async_copy(vel_ref.at[:, :, columns(me)], xv.at[me], local_sem.at[1])
     own_v.start()
+    load_v = pltpu.make_async_copy(vel_ref, vel_out, local_sem.at[5])
+    load_v.start()
     loads = [
         pltpu.make_async_copy(a, b, const_sem.at[i])
         for i, (a, b) in enumerate(
@@ -268,7 +274,8 @@
     def pair_up(c, a, b):
         return jnp.where(lo, a, swap(b)) if c == 0 else jnp.where(lo, swap(a), b)
 
-    load_logc.wait()
+    for copy in early:
+        copy.wait()
     own_p = [
         pltpu.make_async_copy(packed.at[c, me], xp.at[c, me], local_sem.at[2 + c]) for c in range(2)
     ]
@@ -277,7 +284,7 @@
         def pack_psi(to, carry, c=c):
             at = columns(to)
             for p in range(3):
-                packed[c, to, p] = pair_up(c, raw[2 * p, :, at], raw[2 * p + 1, :, at])
+                packed[c, to, p] = pair_up(c, logc_out[2 * p, :, at], logc_out[2 * p + 1, :, at])
             return carry
 
         lax.fori_loop(0, n_dev, pack_psi, 0)
@@ -380,6 +387,16 @@
     for face in faces:
         face.wait()
     every(lambda k, to: send_p(1, k, to, me).start())
+
+    def wall_lanes(layer):
+        lead, trail = lane // NODE_1D % NODE_1D, lane % NODE_1D
+        code = jnp.where(lo, orient_ref[layer * CYCLES], orient_ref[layer * CYCLES + 1])
+        flipped_a = jnp.where(code % 2 == 1, NODE_1D - 1 - lead, lead)
+        flipped_b = jnp.where(code // 2 % 2 == 1, NODE_1D - 1 - trail, trail)
+        x = jnp.where(code // 4 % 2 == 1, flipped_a, flipped_b)
+        inner = jnp.logical_and(lo, x == 0)
+        outer = jnp.logical_and(jnp.logical_not(lo), x == NODE_1D - 1)
+        return inner, jnp.logical_or(inner, outer)
 
     top = lane % NODE_1D == NODE_1D - 1
     low_rows = lane % NODE_1D == 0
@@ -619,125 +636,121 @@
     own = [pltpu.make_async_copy(backs[c].at[me], outs[c].at[me], local_sem.at[c]) for c in range(2)]
     for copy in own:
         copy.start()
+    load_v.wait()
+    mode_ids = me * modes + lax.broadcasted_iota(jnp.int32, (modes, 1), 0)
+    speed = jnp.where(mode_ids == 0, wall_ref[0], 0.0)
+
+    def set_walls(layer, carry):
+        inner, on_wall = wall_lanes(layer)
+        at = columns(layer)
+        for c in range(3):
+            wall = jnp.where(inner, speed, 0.0) if c == 1 else 0.0
+            vel_out[c, :, at] = jnp.where(on_wall, wall, vel_out[c, :, at])
+        return carry
+
+    lax.fori_loop(0, n_dev, set_walls, 0)
     every(lambda k, to: send_v(k, to, me).wait_send())
     for c in range(2):
         every(lambda k, to, c=c: send_p(c, k, to, me).wait_send())
     for copy in own:
         copy.wait()
 
-    def give_wait(k, to):
-        for c in range(2):
-            give(c, to, to).wait_recv()
-            give(c, to, me).wait_send()
-
-    every(give_wait)
-
-
-def final_kernel(
-    n_dev, modes, fold, group,
-    orient_ref, wall_ref, first_ref, second_ref, vel_ref, logc_ref,
-    vel_out, logc_out,
-):
-    step = pl.program_id(0)
-    me = lax.axis_index("mode")
-    lane = lax.broadcasted_iota(jnp.int32, (1, LANES), 1)
-    lo = lane < CELL
-    top = lane % NODE_1D == NODE_1D - 1
-    low_rows = lane % NODE_1D == 0
-    stored = lax.broadcasted_iota(jnp.int32, (LANES, LANES), 0)
     edge = jnp.logical_or(top, low_rows)
-    jump = jnp.where(low_rows, NODE_1D - 1, jnp.where(top, 1 - NODE_1D, 0))
     weight = jnp.where(edge, 0.5 * STEP_DT, STEP_DT)
-    mode_ids = me * modes + lax.broadcasted_iota(jnp.int32, (modes, 1), 0)
-    speed = jnp.where(mode_ids == 0, wall_ref[0], 0.0)
-    cycle = lane // CELL
-    lead = lane // NODE_1D % NODE_1D
-    trail = lane % NODE_1D
-
-    def rolled(value, shift):
-        return pltpu.roll(value, shift % LANES, 1) if shift % LANES else value
-
-    def layer_fields(g):
-        at = lax.rem(step * group + g + n_dev, n_dev)
-        ref0, ref1 = first_ref, second_ref
-        fields = []
-        blocks = [ref0[at, p] if not fold else ref0[at, 4 * p : 4 * p + 4].reshape(modes, LANES) for p in range(3)]
+    joined = jnp.logical_and(lane >= CELL, lane < CELL + NODE_1D)
+
+    def first_fields(at):
         if not fold:
-            blocks.append(ref0[at, 3])
+            blocks = [out0_ref[at, p] for p in range(4)]
         else:
-            units = [ref0[at, 12 + j] for j in range(3)]
+            blocks = [out0_ref[at, 4 * p : 4 * p + 4].reshape(modes, LANES) for p in range(3)]
+            units = [out0_ref[at, 12 + j] for j in range(3)]
             piece = lane // (LANES // 4)
             outer = [rolled(units[j], (j + 1) * (LANES // 4)) for j in range(3)]
             units.append(jnp.where(piece == 0, outer[0], jnp.where(piece == 1, outer[1], outer[2])))
             blocks.append(jnp.concatenate(units, axis=0))
+        fields = []
         for f in range(9):
             b, inside, wall, width = first_cycle(f)
-            shift = wall - inside + (f + 1) % 2 * CELL
-            zero = rolled(blocks[b], shift)
+            value = rolled(blocks[b], wall - inside)
             if inside + width > LANES:
-                zero = jnp.where(lane < shift + LANES, zero, rolled(blocks[b + 1], shift))
+                value = jnp.where(lane < wall + LANES - inside, value, rolled(blocks[b + 1], wall - inside))
+            fields.append(value)
+        return fields
+
+    def second_fields(at):
+        fields = []
+        for f in range(9):
             p = f // 2
             if not fold:
-                one = ref1[at, p]
+                value = rolled(out1_ref[at, p], (f + 1) % 2 * CELL)
             elif p < 4:
-                one = ref1[at, 4 * p : 4 * p + 4].reshape(modes, LANES)
+                value = out1_ref[at, 4 * p : 4 * p + 4].reshape(modes, LANES)
+                value = rolled(value, (f + 1) % 2 * CELL)
             else:
-                one = ref1[at, 16:18].reshape(modes // 2, LANES)
-                one = jnp.concatenate([one, rolled(one, CELL)], axis=0)
-            fields.append(jnp.where(lo, zero, one) if f % 2 else jnp.where(lo, one, zero))
+                value = out1_ref[at, 16:18].reshape(modes // 2, LANES)
+                value = jnp.concatenate([rolled(value, CELL), value], axis=0)
+            fields.append(value)
         return fields
 
-    layers = [layer_fields(g) for g in range(-1, group + 1)]
-    for g in range(group):
-        layer = step * group + g
-        hots = []
-        for nat in ((lane + CELL) % LANES, lane):
-            parts = []
-            for to in (nat, nat + jump):
-                here = jnp.logical_or(nat < KEPT, nat >= CELL)
-                face = jnp.logical_and(nat >= CELL, nat < CELL + NODE_1D)
-                if parts:
-                    here, face = jnp.logical_and(here, edge), jnp.logical_and(face, edge)
-                place = jnp.where(here, stored_index(orient_ref, layer, to), -1)
-                twin = jnp.where(face, stored_index(orient_ref, layer, to - NODE_1D), -1)
-                hit = jnp.logical_or(place == stored, twin == stored)
-                parts += [jnp.where(hit, 1.0, 0.0).astype(BF)] * 2
-            hots.append(jnp.concatenate(parts, axis=1))
-        code = jnp.zeros_like(lane)
-        for c in range(CYCLES):
-            code = jnp.where(cycle == c, orient_ref[layer * CYCLES + c], code)
-        flipped_a = jnp.where(code % 2 == 1, NODE_1D - 1 - lead, lead)
-        flipped_b = jnp.where(code // 2 % 2 == 1, NODE_1D - 1 - trail, trail)
-        x = jnp.where(code // 4 % 2 == 1, flipped_a, flipped_b)
-        inner = jnp.logical_and(cycle == 0, x == 0)
-        outer = jnp.logical_and(cycle == CYCLES - 1, x == NODE_1D - 1)
-        on_wall = jnp.logical_or(inner, outer)
-        cols = slice(g * LANES, (g + 1) * LANES)
-        held = pl.ds(pl.multiple_of(layer * LANES, LANES), LANES)
-        many = modes % 8 == 0
-        for fields in ((0, 2, 4, 6, 8), (1, 3, 5, 7)) if many else [(f,) for f in range(9)]:
-            rates, others = [], []
-            for f in fields:
-                below, rate, above = [layers[g + d][f] for d in range(3)]
-                rates.append(weight * rate)
-                others.append((0.5 * STEP_DT) * jnp.where(top, below, above))
-            pieces = []
-            for part in (rates, others):
-                pieces += split(jnp.concatenate(part, axis=0) if many else part[0])
-            total = lax.dot_general(
-                jnp.concatenate(pieces, axis=1),
-                hots[fields[0] % 2],
-                (((1,), (1,)), ((), ())),
-                preferred_element_type=F32,
-            )
-            for j, f in enumerate(fields):
-                c = CHANNEL_OF[f]
-                own = total[j * modes : (j + 1) * modes]
-                if c < 3:
-                    wall = jnp.where(inner, speed, 0.0) if c == 1 else 0.0
-                    vel_out[c, :, cols] = jnp.where(on_wall, wall, vel_ref[c, :, held] + own)
-                else:
-                    logc_out[c - 3, :, cols] = logc_ref[c - 3, :, held] + own
+    many = modes % 8 == 0
+
+    def add_cycle(c):
+        here = lane >= CELL if c else lane < KEPT
+
+        def add_layer(order, carry):
+            k = 2 * lax.rem(order, side) + order // side
+            frm = target(k)
+
+            @pl.when(k > 0)
+            def _():
+                give(c, frm, frm).wait_recv()
+                give(c, frm, me).wait_send()
+
+            fields = [weight * v for v in (second_fields if c else first_fields)(frm)]
+            step = NODE_1D - 1
+            cats = [jnp.concatenate(split(v), axis=1) for v in ([jnp.concatenate(fields, axis=0)] if many else fields)]
+            layers = [lax.rem(frm + ahead, n_dev) for ahead in (0, 1, n_dev - 1)]
+            hots = []
+            for layer, shift, only in zip(layers, (0, -step, step), (None, top, low_rows)):
+                valid = [v if only is None else jnp.logical_and(v, only) for v in (here, joined)]
+                place = jnp.where(valid[0], stored_index(orient_ref, layer, lane + shift), -1)
+                hit = place == stored
+                if c:
+                    twin = jnp.where(valid[1], stored_index(orient_ref, layer, lane + shift - NODE_1D), -1)
+                    hit = jnp.logical_or(hit, twin == stored)
+                hot = jnp.where(hit, 1.0, 0.0).astype(BF)
+                hots.append(jnp.concatenate([hot, hot], axis=1))
+            hots = jnp.concatenate(hots, axis=0)
+            sums = [
+                lax.dot_general(v, hots, (((1,), (1,)), ((), ())), preferred_element_type=F32) for v in cats
+            ]
+            for j, layer in enumerate(layers):
+                _, on_wall = wall_lanes(layer)
+                at = columns(layer)
+                cols = slice(j * LANES, (j + 1) * LANES)
+                for f in range(9):
+                    total = sums[0][f * modes : (f + 1) * modes, cols] if many else sums[f][:, cols]
+                    to = CHANNEL_OF[f]
+                    if to < 3:
+                        vel_out[to, :, at] += jnp.where(on_wall, 0.0, total)
+                    else:
+                        logc_out[to - 3, :, at] += total
+            return carry
+
+        lax.fori_loop(0, n_dev, add_layer, 0)
+
+    add_cycle(0)
+    add_cycle(1)
+
+
+def store_kernel(vel_ref, logc_ref, vel_out, logc_out, sem):
+    copies = [pltpu.make_async_copy(vel_ref.at[c], vel_out.at[c], sem.at[c]) for c in range(3)]
+    copies += [pltpu.make_async_copy(logc_ref.at[c], logc_out.at[c], sem.at[3 + c]) for c in range(6)]
+    for copy in copies:
+        copy.start()
+    for copy in copies:
+        copy.wait()
 
 
 def body(velocity, log_conf, orientation, wall_speed):
@@ -748,21 +761,22 @@
     tail = (18, modes // 4, LANES) if fold else (5, modes, LANES)
     consts = [jnp.asarray(t) for t in tables()]
     hbm = pl.BlockSpec(memory_space=pltpu.HBM)
-    free = pl.BlockSpec(memory_space=pl.ANY)
-    smem = pl.BlockSpec(memory_space=pltpu.SMEM)
+    vmem = pl.BlockSpec(memory_space=pltpu.VMEM)
     dma = pltpu.SemaphoreType.DMA
     face_rows = PLANES + PLANES * CYCLES * NODE_1D // LANES
-    first, second = pl.pallas_call(
+    held = pl.pallas_call(
         functools.partial(main_kernel, n_dev, modes, fold),
         out_shape=(
-            jax.ShapeDtypeStruct((n_dev, *head), F32),
-            jax.ShapeDtypeStruct((n_dev, *tail), F32),
+            jax.ShapeDtypeStruct(velocity.shape, F32),
+            jax.ShapeDtypeStruct(log_conf.shape, F32),
         ),
-        in_specs=[hbm, hbm, smem] + [hbm] * len(consts),
-        out_specs=(free, free),
+        in_specs=[hbm] * 3 + [pl.BlockSpec(memory_space=pltpu.SMEM)] + [hbm] * len(consts),
+        out_specs=(vmem, vmem),
         scratch_shapes=[pltpu.VMEM(t.shape, t.dtype) for t in consts]
         + [
-            pltpu.VMEM(log_conf.shape, F32),
+            pltpu.SMEM(orientation.shape, jnp.int32),
+            pltpu.VMEM((n_dev, *head), F32),
+            pltpu.VMEM((n_dev, *tail), F32),
             pltpu.VMEM((2, n_dev, 3, modes, LANES), F32),
             pltpu.VMEM((n_dev, 3, modes, LANES), F32),
             pltpu.VMEM((2, n_dev, 3, modes, LANES), F32),
@@ -785,7 +799,7 @@
             pltpu.VMEM((5, PLANES, LANES), F32),
             pltpu.VMEM((n_dev, *head), F32),
             pltpu.VMEM((n_dev, *tail), F32),
-            dma((4,)),
+            dma((6,)),
             dma((len(consts),)),
             dma((n_dev,)),
             dma((n_dev,)),
@@ -800,34 +814,25 @@
             collective_id=0, has_side_effects=True, vmem_limit_bytes=36 * 2**20
         ),
         name="fields",
-    )(*[pltpu.with_memory_space_constraint(v, pltpu.HBM) for v in (velocity, log_conf, orientation, *consts)])
-
-    group = 8
-    tile = group * LANES
-
-    vmem = pl.BlockSpec(memory_space=pltpu.VMEM)
+    )(
+        *[pltpu.with_memory_space_constraint(v, pltpu.HBM) for v in (velocity, log_conf, orientation)],
+        wall_speed,
+        *[pltpu.with_memory_space_constraint(v, pltpu.HBM) for v in consts],
+    )
+
+    free = pl.BlockSpec(memory_space=pl.ANY)
     return pl.pallas_call(
-        functools.partial(final_kernel, n_dev, modes, fold, group),
-        grid=(n_dev // group,),
+        store_kernel,
         out_shape=(
             jax.ShapeDtypeStruct(velocity.shape, F32),
             jax.ShapeDtypeStruct(log_conf.shape, F32),
         ),
-        in_specs=[
-            smem,
-            smem,
-            vmem,
-            vmem,
-            vmem,
-            vmem,
-        ],
-        out_specs=(
-            pl.BlockSpec((3, modes, tile), lambda i: (0, 0, i)),
-            pl.BlockSpec((6, modes, tile), lambda i: (0, 0, i)),
-        ),
-        compiler_params=pltpu.CompilerParams(vmem_limit_bytes=24 * 2**20),
-        name="finish",
-    )(pltpu.with_memory_space_constraint(orientation, pltpu.HBM), wall_speed, first, second, velocity, log_conf)
+        in_specs=[vmem, vmem],
+        out_specs=(free, free),
+        scratch_shapes=[dma((9,))],
+        compiler_params=pltpu.CompilerParams(vmem_limit_bytes=8 * 2**20),
+        name="store",
+    )(*held)
 
 
 def solution(mesh):

time: 116 us -> 115 us (level)
  Pallas kernels: 115 us -> 113 us
    pallas_call x1, Pallas kernels: 4.59 us -> 1.47 us  [body(): pl.pallas_call(store_kernel, out_shape=(jax.ShapeDtypeStruct(velocity.sha...]
    pallas_call x1, Pallas kernels: 110 us -> 112 us  [body(): pl.pallas_call(functools.partial(main_kernel, n_dev, modes, fold), out_sh...]
where the time goes in v4:
time: 115 us; the launch traced here: 114 us
  Pallas kernels  113 us (98%)
  between operations  1.28 us (1%)
    pallas_call x1, Pallas kernels, body(): pl.pallas_call(functools.partial(main_kernel, n_dev, modes, fold), out_sh...  112 us

profile of v4, /device:TPU:15, one launch (start us, length us, event | category | flops | bytes accessed | tf_op | source)
XLA Modules:
  0.0 114.5 jit_solution(15701757174028274608)
XLA Ops:
  1.3 111.7 %fields.1 = (f32[3,32,2048]{2,1,0:T(8,128)S(1)}, f32[6,32,2048]{2,1,0:T(8,128)S(1)}) custom-call(f32[3,32,2048]{2,1,0:T(8,128)} %vel_ref.1, f32[6,32,2048]{2,1,0:T(8,128)} %logc_ref.1, s32[32]{0:T(128)} %orient_in.1, f32[1]{0:T(128)S(6)} %copy.12.wall_ref, bf16[1024,512]{1,0:T(8,128)(2,1)} %constant.12.clone.fh_in, bf16[1024,512]{1,0:T(8,128)(2,1)} %constant.13.clone.fl_in, ...), custom_call_target="tpu_custom_call" | custom-call | tf_op jit(solution)/shard_map/fields/pallas_call | solution.py:767
  113.0 1.5 %store.1 = (f32[3,32,2048]{2,1,0:T(8,128)}, f32[6,32,2048]{2,1,0:T(8,128)}) custom-call(f32[3,32,2048]{2,1,0:T(8,128)S(1)} %get-tuple-element.4.vel_ref, f32[6,32,2048]{2,1,0:T(8,128)S(1)} %get-tuple-element.5.logc_ref), custom_call_target="tpu_custom_call" | custom-call | tf_op jit(solution)/shard_map/store/pallas_call | solution.py:824

commit v5 on v4

--- a/solution.py
+++ b/solution.py
@@ -699,10 +699,13 @@
         here = lane >= CELL if c else lane < KEPT
 
         def add_layer(order, carry):
-            k = 2 * lax.rem(order, side) + order // side
-            frm = target(k)
-
-            @pl.when(k > 0)
+            far = order // side
+            m = lax.rem(order, side)
+            local = lax.rem(me, side)
+            near_by = lax.rem(local // per + m // per, 2) * per + lax.rem(local + n_dev * per - m, per)
+            frm = lax.rem(half_of + far, 2) * side + near_by
+
+            @pl.when(order > 0)
             def _():
                 give(c, frm, frm).wait_recv()
                 give(c, frm, me).wait_send()

time: 115 us -> 112 us (0.974)
  Pallas kernels: 113 us -> 111 us
    pallas_call x1, Pallas kernels: 112 us -> 109 us  [body(): pl.pallas_call(functools.partial(main_kernel, n_dev, modes, fold), out_sh...]
where the time goes in v5:
time: 112 us
  Pallas kernels  111 us (99%)
  between operations  1.28 us (1%)
    pallas_call x1, Pallas kernels, body(): pl.pallas_call(functools.partial(main_kernel, n_dev, modes, fold), out_sh...  109 us

profile of v5, /device:TPU:15, one launch (start us, length us, event | category | flops | bytes accessed | tf_op | source)
XLA Modules:
  0.0 112.1 jit_solution(3499068883037768724)
XLA Ops:
  1.3 109.3 %fields.1 = (f32[3,32,2048]{2,1,0:T(8,128)S(1)}, f32[6,32,2048]{2,1,0:T(8,128)S(1)}) custom-call(f32[3,32,2048]{2,1,0:T(8,128)} %vel_ref.1, f32[6,32,2048]{2,1,0:T(8,128)} %logc_ref.1, s32[32]{0:T(128)} %orient_in.1, f32[1]{0:T(128)S(6)} %copy.12.wall_ref, bf16[1024,512]{1,0:T(8,128)(2,1)} %constant.12.clone.fh_in, bf16[1024,512]{1,0:T(8,128)(2,1)} %constant.13.clone.fl_in, ...), custom_call_target="tpu_custom_call" | custom-call | tf_op jit(solution)/shard_map/fields/pallas_call | solution.py:770
  110.6 1.5 %store.1 = (f32[3,32,2048]{2,1,0:T(8,128)}, f32[6,32,2048]{2,1,0:T(8,128)}) custom-call(f32[3,32,2048]{2,1,0:T(8,128)S(1)} %get-tuple-element.4.vel_ref, f32[6,32,2048]{2,1,0:T(8,128)S(1)} %get-tuple-element.5.logc_ref), custom_call_target="tpu_custom_call" | custom-call | tf_op jit(solution)/shard_map/store/pallas_call | solution.py:827

commit v6 on v5

--- a/solution.py
+++ b/solution.py
@@ -386,7 +386,14 @@
 
     for face in faces:
         face.wait()
-    every(lambda k, to: send_p(1, k, to, me).start())
+    def far_or_near(far):
+        def step(k, carry):
+            send_p(1, 2 * k + far, target(2 * k + far), me).start()
+            return carry
+
+        lax.fori_loop(1 - far, side, step, 0)
+
+    far_or_near(1)
 
     def wall_lanes(layer):
         lead, trail = lane // NODE_1D % NODE_1D, lane % NODE_1D
@@ -483,6 +490,8 @@
         own_p[c].wait()
         recv_half(0)
         conf_half(0)
+        if c == 0:
+            far_or_near(0)
         recv_half(1)
         conf_half(1)
 

time: 112 us -> 111 us (level)
  Pallas kernels: 111 us -> 109 us
    pallas_call x1, Pallas kernels: 109 us -> 108 us  [body(): pl.pallas_call(functools.partial(main_kernel, n_dev, modes, fold), out_sh...]
where the time goes in v6:
time: 111 us; the launch traced here: 110 us
  Pallas kernels  109 us (98%)
  between operations  1.28 us (1%)
    pallas_call x1, Pallas kernels, body(): pl.pallas_call(functools.partial(main_kernel, n_dev, modes, fold), out_sh...  108 us

profile of v6, /device:TPU:15, one launch (start us, length us, event | category | flops | bytes accessed | tf_op | source)
XLA Modules:
  0.0 110.5 jit_solution(999936631353356718)
XLA Ops:
  1.3 107.7 %fields.1 = (f32[3,32,2048]{2,1,0:T(8,128)S(1)}, f32[6,32,2048]{2,1,0:T(8,128)S(1)}) custom-call(f32[3,32,2048]{2,1,0:T(8,128)} %vel_ref.1, f32[6,32,2048]{2,1,0:T(8,128)} %logc_ref.1, s32[32]{0:T(128)} %orient_in.1, f32[1]{0:T(128)S(6)} %copy.12.wall_ref, bf16[1024,512]{1,0:T(8,128)(2,1)} %constant.12.clone.fh_in, bf16[1024,512]{1,0:T(8,128)(2,1)} %constant.13.clone.fl_in, ...), custom_call_target="tpu_custom_call" | custom-call | tf_op jit(solution)/shard_map/fields/pallas_call | solution.py:779
  109.0 1.5 %store.1 = (f32[3,32,2048]{2,1,0:T(8,128)}, f32[6,32,2048]{2,1,0:T(8,128)}) custom-call(f32[3,32,2048]{2,1,0:T(8,128)S(1)} %get-tuple-element.4.vel_ref, f32[6,32,2048]{2,1,0:T(8,128)S(1)} %get-tuple-element.5.logc_ref), custom_call_target="tpu_custom_call" | custom-call | tf_op jit(solution)/shard_map/store/pallas_call | solution.py:836

commit v7 on v6

--- a/solution.py
+++ b/solution.py
@@ -490,9 +490,9 @@
         own_p[c].wait()
         recv_half(0)
         conf_half(0)
+        recv_half(1)
         if c == 0:
             far_or_near(0)
-        recv_half(1)
         conf_half(1)
 
         def deriv_block(i, carry):

time: 111 us -> 111 us (level)
  no operation moved by 1% of the time
where the time goes in v7:
time: 111 us; the launch traced here: 110 us
  Pallas kernels  109 us (98%)
  between operations  1.28 us (1%)
    pallas_call x1, Pallas kernels, body(): pl.pallas_call(functools.partial(main_kernel, n_dev, modes, fold), out_sh...  108 us

profile of v7, /device:TPU:15, one launch (start us, length us, event | category | flops | bytes accessed | tf_op | source)
XLA Modules:
  0.0 110.5 jit_solution(15055325584745391734)
XLA Ops:
  1.3 107.7 %fields.1 = (f32[3,32,2048]{2,1,0:T(8,128)S(1)}, f32[6,32,2048]{2,1,0:T(8,128)S(1)}) custom-call(f32[3,32,2048]{2,1,0:T(8,128)} %vel_ref.1, f32[6,32,2048]{2,1,0:T(8,128)} %logc_ref.1, s32[32]{0:T(128)} %orient_in.1, f32[1]{0:T(128)S(6)} %copy.12.wall_ref, bf16[1024,512]{1,0:T(8,128)(2,1)} %constant.12.clone.fh_in, bf16[1024,512]{1,0:T(8,128)(2,1)} %constant.13.clone.fl_in, ...), custom_call_target="tpu_custom_call" | custom-call | tf_op jit(solution)/shard_map/fields/pallas_call | solution.py:779
  109.0 1.5 %store.1 = (f32[3,32,2048]{2,1,0:T(8,128)}, f32[6,32,2048]{2,1,0:T(8,128)}) custom-call(f32[3,32,2048]{2,1,0:T(8,128)S(1)} %get-tuple-element.4.vel_ref, f32[6,32,2048]{2,1,0:T(8,128)S(1)} %get-tuple-element.5.logc_ref), custom_call_target="tpu_custom_call" | custom-call | tf_op jit(solution)/shard_map/store/pallas_call | solution.py:836
